TPU v7x, 32 devices: a whole 2x2x4 slice. The times are simulated.
32 devices in a mesh: expert: 16 (over z, y, core), dp: 2 (over x).
Axes of the slice: x: 2, y: 2, z: 4, core: 2. Of those that a mesh axis runs over, the one named last changes fastest.
Arguments:
- tokens: bfloat16 [2048, 2048], P('expert', 'dp'), may hold values from -6 to 6
- grad_out: bfloat16 [2048, 2048], P('expert', 'dp'), may hold values from -6 to 6
- routes: int32 [2048, 8], P('expert'), may hold values from 0 to 15, all different within a row; in each aligned block of 128 rows (0 to 127, 128 to 255, ...) at most 96 rows name the same one
- gates: float32 [2048, 8], P('expert'), may hold values from 0.1 to 1
- w_gate: bfloat16 [16, 2048, 384], P('expert', 'dp'), may hold values from -0.125 to 0.125
- w_up: bfloat16 [16, 2048, 384], P('expert', 'dp'), may hold values from -0.125 to 0.125
- w_down: bfloat16 [16, 384, 2048], P('expert', None, 'dp'), may hold values from -0.3125 to 0.3125
Outputs:
- d_tokens: bfloat16 [2048, 2048], P('expert', 'dp')
- grad_gate: bfloat16 [16, 2048, 384], P('expert', 'dp')
- grad_up: bfloat16 [16, 2048, 384], P('expert', 'dp')
- grad_down: bfloat16 [16, 384, 2048], P('expert', None, 'dp')
Inputs may be any that keep to these rules, and one draw needn't show every extreme that they name: `routes`: each row names 8 different experts; in each aligned block of 128 rows no expert is named by more than 96 rows, a bound that some block reaches.
All inputs are finite; a program needn't handle non-finite values.
Results may differ from a plain program's by a relative error of at most 0.013.
Values may be sent and summed in bfloat16 or wider, within the bound.
A program may use at most 64 MiB of HBM per device.

v0:
```python
import jax
import jax.numpy as jnp
from jax import lax
from jax.sharding import PartitionSpec as P


def contract_rows(left_rows, right_rows):
    return lax.dot_general(
        left_rows, right_rows, (((0,), (0,)), ((), ())), preferred_element_type=jnp.float32
    )


def contract_cols(left_rows, right_rows):
    return lax.dot_general(
        left_rows, right_rows, (((1,), (1,)), ((), ())), preferred_element_type=jnp.float32
    )


def per_source(left_rows, right_rows, dp_count):
    left_split = left_rows.reshape(dp_count, -1, left_rows.shape[1])
    right_split = right_rows.reshape(dp_count, -1, right_rows.shape[1])
    partial_value = jnp.einsum(
        "jra,jrb->jab", left_split, right_split, preferred_element_type=jnp.float32
    )
    rounded = lax.optimization_barrier(partial_value.astype(jnp.bfloat16))
    return jnp.sum(rounded.astype(jnp.float32), axis=0).astype(jnp.bfloat16)


def shards(tokens, grad_out, routes, gates, w_gate, w_up, w_down):
    experts = lax.axis_size("expert")
    dp_count = lax.axis_size("dp")
    tok_count = tokens.shape[0]
    top_count = routes.shape[1]
    slot_cap = min(tok_count, max(2, 3 * tok_count * top_count // (2 * experts)))
    row_total = tok_count * top_count
    flat_routes = routes.reshape(-1)
    flat_gates = gates.reshape(-1)
    onehot = (flat_routes[:, None] == jnp.arange(experts, dtype=jnp.int32)[None, :]).astype(
        jnp.int32
    )
    slot_rank = jnp.sum((jnp.cumsum(onehot, axis=0) - onehot) * onehot, axis=1)
    slot_index = flat_routes * slot_cap + slot_rank
    slot_source = (
        jnp.full((experts * slot_cap,), row_total, jnp.int32)
        .at[slot_index]
        .set(jnp.arange(row_total, dtype=jnp.int32))
    )
    valid = slot_source < row_total
    safe_rows = jnp.where(valid, slot_source, 0)
    token_ids = safe_rows // top_count
    token_slots = jnp.where(valid[:, None], tokens[token_ids], jnp.zeros((), tokens.dtype))
    scaled_slots = jnp.where(
        valid[:, None],
        grad_out[token_ids].astype(jnp.float32) * flat_gates[safe_rows][:, None],
        0.0,
    ).astype(jnp.bfloat16)
    input_cols, scaled_cols = (
        lax.all_to_all(token_slots, "expert", split_axis=0, concat_axis=0, tiled=True),
        lax.all_to_all(scaled_slots, "expert", split_axis=0, concat_axis=0, tiled=True),
    )
    inputs, scaled = (
        lax.all_to_all(input_cols, "dp", split_axis=0, concat_axis=1, tiled=True),
        lax.all_to_all(scaled_cols, "dp", split_axis=0, concat_axis=1, tiled=True),
    )
    full_gate, full_up, full_down = (
        lax.all_gather(w_gate, "dp", axis=1, tiled=True),
        lax.all_gather(w_up, "dp", axis=1, tiled=True),
        lax.all_gather(w_down, "dp", axis=2, tiled=True),
    )
    full_gate = full_gate[0]
    full_up = full_up[0]
    full_down = full_down[0]
    pre_gate = jnp.dot(inputs, full_gate, preferred_element_type=jnp.float32)
    pre_up = jnp.dot(inputs, full_up, preferred_element_type=jnp.float32)
    sigmoid_gate = jax.nn.sigmoid(pre_gate)
    activated = pre_gate * sigmoid_gate
    hidden = (activated * pre_up).astype(jnp.bfloat16)
    back_hidden = contract_cols(scaled, full_down)
    d_up = (back_hidden * activated).astype(jnp.bfloat16)
    d_gate = (back_hidden * pre_up * sigmoid_gate * (1.0 + pre_gate * (1.0 - sigmoid_gate))).astype(
        jnp.bfloat16
    )
    row_grad = (contract_cols(d_gate, full_gate) + contract_cols(d_up, full_up)).astype(
        jnp.bfloat16
    )
    came_back = lax.all_to_all(
        lax.all_to_all(row_grad, "dp", split_axis=1, concat_axis=0, tiled=True),
        "expert",
        split_axis=0,
        concat_axis=0,
        tiled=True,
    )
    picked = came_back[slot_index].astype(jnp.float32)
    d_tokens = jnp.sum(picked.reshape(tok_count, top_count, -1), axis=1).astype(jnp.bfloat16)
    hidden_all = lax.all_gather(hidden, "dp", axis=0, tiled=True)
    grad_down = per_source(hidden_all, scaled_cols, dp_count)
    gate_part = contract_rows(inputs, d_gate).astype(jnp.bfloat16).astype(jnp.float32)
    up_part = contract_rows(inputs, d_up).astype(jnp.bfloat16).astype(jnp.float32)
    gate_sum, up_sum = (
        lax.psum_scatter(
            gate_part.astype(jnp.bfloat16), "dp", scatter_dimension=0, tiled=True
        ).astype(jnp.float32),
        lax.psum_scatter(
            up_part.astype(jnp.bfloat16), "dp", scatter_dimension=0, tiled=True
        ).astype(jnp.float32),
    )
    grad_gate = gate_sum.astype(jnp.bfloat16)
    grad_up = up_sum.astype(jnp.bfloat16)
    return (d_tokens, grad_gate[None], grad_up[None], grad_down[None])


def solution(mesh):
    return jax.shard_map(
        shards,
        mesh=mesh,
        in_specs=(
            P("expert", "dp"),
            P("expert", "dp"),
            P("expert", None),
            P("expert", None),
            P("expert", "dp", None),
            P("expert", "dp", None),
            P("expert", None, "dp"),
        ),
        out_specs=(
            P("expert", "dp"),
            P("expert", "dp", None),
            P("expert", "dp", None),
            P("expert", None, "dp"),
        ),
        check_vma=False,
    )
```

profile of v0, /device:TPU:25, one launch (start us, length us, event | category | flops | bytes accessed | tf_op | source)
XLA Modules:
  0.0 458.4 jit_solution(10562967382833381605)
XLA Ops:
  7.2 0.0 copy-start
  7.2 0.7 broadcast_multiply_fusion
  7.9 0.8 copy.24
  8.7 0.1 eq.29
  8.8 0.1 eq.25
  8.9 0.1 copy.23
  9.0 0.1 mul.53
  9.1 4.5 reduce-window.6
  13.6 0.1 slice.16
  13.7 0.1 copy.26
  13.9 0.1 copy.27
  13.9 0.1 broadcast_add_fusion
  14.1 4.3 scatter_custom_fusion
  18.5 0.1 broadcast_in_dim.50
  18.6 5.1 %gather_fusion.2 = bf16[1536,1024]{1,0:T(8,128)(2,1)S(1)} fusion(bf16[128,1024]{1,0:T(8,128)(2,1)S(1)} %copy-done, s32[2048]{0:T(1024)S(1)} %get-tuple-element.10), kind=kCustom, calls=%fused_computation.2 | custom fusion | bytes 6297600 | tf_op jit(solution)/shard_map/gather | solution.py:51
  23.6 1.9 broadcast_select_fusion
  25.5 6.5 %all-to-all-start.2 = ((bf16[16,96,1024]{2,1,0:T(8,128)(2,1)}), bf16[16,96,1024]{2,1,0:T(8,128)(2,1)}, u32[]{:S(2)}, u32[]{:S(2)}) async-start(bf16[16,96,1024]{2,1,0:T(8,128)(2,1)} %broadcast_select_fusion), calls=%async_computation.2 | async-start | bytes 6291456 | tf_op jit(solution)/shard_map/all_to_all | solution.py:58
  32.0 0.1 copy.28
  32.1 0.1 reshape.103
  32.2 0.0 copy-start.2
  32.2 5.9 %gather_fusion.1 = f32[1536]{0:T(1024)S(1)} fusion(f32[1024]{0:T(1024)S(1)} %reshape.103, s32[2048]{0:T(1024)S(1)} %get-tuple-element.9), kind=kCustom, calls=%fused_computation.1 | custom fusion | bytes 18432 | tf_op jit(solution)/shard_map/gather | solution.py:54
  38.1 0.1 mul.55
  38.2 5.1 %gather_fusion = bf16[1536,1024]{1,0:T(8,128)(2,1)S(1)} fusion(bf16[128,1024]{1,0:T(8,128)(2,1)S(1)} %copy-done.2, s32[2048]{0:T(1024)S(1)} %get-tuple-element.10), kind=kCustom, calls=%fused_computation | custom fusion | bytes 6297600 | tf_op jit(solution)/shard_map/gather | solution.py:54
  43.2 2.2 fusion.1
  45.4 51.9 %all-to-all-done.2 = bf16[16,96,1024]{2,1,0:T(8,128)(2,1)} async-done(((bf16[16,96,1024]{2,1,0:T(8,128)(2,1)}), bf16[16,96,1024]{2,1,0:T(8,128)(2,1)}, u32[]{:S(2)}, u32[]{:S(2)}) %all-to-all-start.2) | async-done | bytes 3145760 | tf_op jit(solution)/shard_map/all_to_all | solution.py:58
  97.3 9.6 %all-to-all-start = ((bf16[16,96,1024]{2,1,0:T(8,128)(2,1)}), bf16[16,96,1024]{2,1,0:T(8,128)(2,1)}, u32[]{:S(2)}, u32[]{:S(2)}) async-start(bf16[16,96,1024]{2,1,0:T(8,128)(2,1)} %fusion.1), calls=%async_computation | async-start | bytes 6291456 | tf_op jit(solution)/shard_map/all_to_all | solution.py:59
  106.9 0.0 all-gather.5.cloned.1.call-start
  107.0 0.7 all-gather.5.cloned.1.call-update
  107.7 64.6 %all-to-all-done = bf16[16,96,1024]{2,1,0:T(8,128)(2,1)} async-done(((bf16[16,96,1024]{2,1,0:T(8,128)(2,1)}), bf16[16,96,1024]{2,1,0:T(8,128)(2,1)}, u32[]{:S(2)}, u32[]{:S(2)}) %all-to-all-start) | async-done | bytes 3145760 | tf_op jit(solution)/shard_map/all_to_all | solution.py:59
  172.2 3.9 all-to-all-start.3
  176.2 0.0 all-gather.9.cloned.1.call-start
  176.2 0.7 all-gather.9.cloned.1.call-update
  176.9 52.5 %all-to-all-done.3 = bf16[2,768,1024]{2,1,0:T(8,128)(2,1)S(1)} async-done(((bf16[2,768,1024]{2,1,0:T(8,128)(2,1)}), bf16[2,768,1024]{2,1,0:T(8,128)(2,1)S(1)}, u32[]{:S(2)}, u32[]{:S(2)}) %all-to-all-start.3) | async-done | bytes 3145760 | tf_op jit(solution)/shard_map/all_to_all | solution.py:62
  229.4 1.7 copy-done.4
  231.1 5.2 %all-to-all-start.1 = ((bf16[2,768,1024]{2,1,0:T(8,128)(2,1)}), bf16[2,768,1024]{2,1,0:T(8,128)(2,1)}, u32[]{:S(2)}, u32[]{:S(2)}) async-start(bf16[2,768,1024]{2,1,0:T(8,128)(2,1)} %bitcast.5), calls=%async_computation.1 | async-start | bytes 6291456 | tf_op jit(solution)/shard_map/all_to_all | solution.py:63
  236.3 0.2 all-gather.7.cloned.1.call-start
  236.6 0.5 all-gather.7.cloned.1.call-update
  237.1 3.2 copy.30
  240.3 0.0 copy-start.3
  240.3 48.6 %all-to-all-done.1 = bf16[2,768,1024]{2,1,0:T(8,128)(2,1)} async-done(((bf16[2,768,1024]{2,1,0:T(8,128)(2,1)}), bf16[2,768,1024]{2,1,0:T(8,128)(2,1)}, u32[]{:S(2)}, u32[]{:S(2)}) %all-to-all-start.1) | async-done | bytes 3145760 | tf_op jit(solution)/shard_map/all_to_all | solution.py:63
  288.8 4.6 %copy.29 = bf16[768,2,1024]{0,2,1:T(8,128)(2,1)} copy(bf16[768,2,1024]{2,0,1:T(8,128)(2,1)} %bitcast.6) | data formatting | bytes 6291456 | tf_op jit(solution)/shard_map/all_to_all | solution.py:63
  293.5 5.2 %fusion.9 = f32[768,384]{1,0:T(8,128)} fusion(bf16[768,2048]{0,1:T(8,128)(2,1)} %bitcast.80, bf16[1,384,2048]{2,1,0:T(8,128)(2,1)} %all-gather.5.cloned.1.call-done), kind=kOutput, calls=%fused_computation.22 | convolution fusion | flops 1207959552 | bytes 5898240 | tf_op jit(solution)/shard_map/dot_general | solution.py:14
  298.7 4.2 fusion.4
  302.9 5.2 %multiply_convert_fusion = (bf16[768,384]{1,0:T(8,128)(2,1)}, bf16[768,384]{1,0:T(8,128)(2,1)S(1)}, bf16[768,384]{1,0:T(8,128)(2,1)S(1)}) fusion(f32[768,384]{1,0:T(8,128)} %fusion.4, f32[768,384]{1,0:T(8,128)} %fusion.9, bf16[768,2048]{0,1:T(8,128)(2,1)S(1)} %bitcast.72, bf16[1,2048,384]{2,1,0:T(8,128)(2,1)} %all-gather.7.cloned.1.call-done), kind=kOutput, calls=%fused_computation.24 | convolution fusion | flops 1212383232 | bytes 8847360 | tf_op jit(solution)/shard_map/dot_general | solution.py:74
  308.1 1.8 fusion.2
  310.0 1.8 add_convert_fusion
  311.8 2.0 copy.38
  313.8 5.2 %all-to-all-start.4 = ((bf16[768,2,1024]{2,0,1:T(8,128)(2,1)}), bf16[768,2,1024]{2,0,1:T(8,128)(2,1)}, u32[]{:S(2)}, u32[]{:S(2)}) async-start(bf16[768,2,1024]{2,0,1:T(8,128)(2,1)} %bitcast.76), calls=%async_computation.4 | async-start | bytes 6291456 | tf_op jit(solution)/shard_map/all_to_all | solution.py:87
  319.0 0.0 all-gather.11.cloned.1.call-start
  319.1 0.5 all-gather.11.cloned.1.call-update
  319.6 0.0 reduce-scatter.5.cloned.1.call-start
  319.6 4.0 convolution_convert_fusion
  323.7 0.0 reduce-scatter.5.cloned.1.call-update
  323.7 42.7 %all-to-all-done.4 = bf16[768,2,1024]{2,0,1:T(8,128)(2,1)} async-done(((bf16[768,2,1024]{2,0,1:T(8,128)(2,1)}), bf16[768,2,1024]{2,0,1:T(8,128)(2,1)}, u32[]{:S(2)}, u32[]{:S(2)}) %all-to-all-start.4) | async-done | bytes 3145760 | tf_op jit(solution)/shard_map/all_to_all | solution.py:87
  366.4 10.9 %all-to-all-start.5 = ((bf16[16,96,1024]{2,1,0:T(8,128)(2,1)}), bf16[16,96,1024]{2,1,0:T(8,128)(2,1)S(1)}, u32[]{:S(2)}, u32[]{:S(2)}) async-start(bf16[16,96,1024]{2,1,0:T(8,128)(2,1)} %bitcast.16), calls=%async_computation.5 | async-start | bytes 6291456 | tf_op jit(solution)/shard_map/all_to_all | solution.py:86
  377.2 0.3 reduce-scatter.3.cloned.1.call-start
  377.5 5.0 %convolution_convert_fusion.1 = bf16[2048,384]{1,0:T(8,128)(2,1)} fusion(bf16[768,2048]{0,1:T(8,128)(2,1)} %bitcast.74, bf16[768,384]{1,0:T(8,128)(2,1)} %copy-done.7), kind=kOutput, calls=%fused_computation.12 | convolution fusion | flops 1208745984 | bytes 5308416 | tf_op jit(solution)/shard_map/dot_general | solution.py:8
  382.5 0.0 reduce-scatter.3.cloned.1.call-update
  382.6 0.0 all-gather.11.cloned.1.call-done
  382.6 4.9 %convolution_convert_fusion.2 = bf16[2,384,1024]{2,1,0:T(8,128)(2,1)} fusion(bf16[2,768,384]{2,1,0:T(8,128)(2,1)} %bitcast.87, bf16[2,768,1024]{2,1,0:T(8,128)(2,1)} %bitcast.5), kind=kOutput, calls=%fused_computation.14 | convolution fusion | flops 1208745984 | bytes 5898240 | tf_op jit(solution)/shard_map/jra,jrb->jab/dot_general | solution.py:22
  387.5 2.9 reduce_sum.38
  390.3 52.1 %all-to-all-done.5 = bf16[16,96,1024]{2,1,0:T(8,128)(2,1)S(1)} async-done(((bf16[16,96,1024]{2,1,0:T(8,128)(2,1)}), bf16[16,96,1024]{2,1,0:T(8,128)(2,1)S(1)}, u32[]{:S(2)}, u32[]{:S(2)}) %all-to-all-start.5) | async-done | bytes 3145760 | tf_op jit(solution)/shard_map/all_to_all | solution.py:86
  442.4 5.4 %gather_fusion.3 = bf16[1024,1024]{1,0:T(8,128)(2,1)} fusion(bf16[1536,1024]{1,0:T(8,128)(2,1)S(1)} %bitcast.70, s32[1024]{0:T(1024)S(1)} %broadcast_clamp_fusion), kind=kCustom, calls=%fused_computation.3 | custom fusion | bytes 4198400 | tf_op jit(solution)/shard_map/gather | solution.py:93
  447.8 3.7 bitcast_reduce_fusion
  (31 shorter events, 0.1 us)
Async XLA Ops:
  7.2 11.4 %copy-start = (bf16[128,1024]{1,0:T(8,128)(2,1)S(1)}, bf16[128,1024]{1,0:T(8,128)(2,1)}, u32[]{:S(2)}) copy-start(bf16[128,1024]{1,0:T(8,128)(2,1)} %param.7) | copy-start | bytes 786436
  25.5 6.5 %copy-start.9 = (f32[128,8]{0,1:T(8,128)S(1)}, f32[128,8]{0,1:T(8,128)}, u32[]{:S(2)}) copy-start(f32[128,8]{0,1:T(8,128)} %param.10) | copy-start | bytes 12292
  25.5 71.8 %all-to-all-start.2 = ((bf16[16,96,1024]{2,1,0:T(8,128)(2,1)}), bf16[16,96,1024]{2,1,0:T(8,128)(2,1)}, u32[]{:S(2)}, u32[]{:S(2)}) async-start(bf16[16,96,1024]{2,1,0:T(8,128)(2,1)} %broadcast_select_fusion), calls=%async_computation.2 | async-start | bytes 6291456 | tf_op jit(solution)/shard_map/all_to_all | solution.py:58
  32.2 5.9 %copy-start.2 = (bf16[128,1024]{1,0:T(8,128)(2,1)S(1)}, bf16[128,1024]{1,0:T(8,128)(2,1)}, u32[]{:S(2)}) copy-start(bf16[128,1024]{1,0:T(8,128)(2,1)} %param.8) | copy-start | bytes 786436
  97.3 74.9 %all-to-all-start = ((bf16[16,96,1024]{2,1,0:T(8,128)(2,1)}), bf16[16,96,1024]{2,1,0:T(8,128)(2,1)}, u32[]{:S(2)}, u32[]{:S(2)}) async-start(bf16[16,96,1024]{2,1,0:T(8,128)(2,1)} %fusion.1), calls=%async_computation | async-start | bytes 6291456 | tf_op jit(solution)/shard_map/all_to_all | solution.py:59
  106.9 186.5 %all-gather.5.cloned.1.call-start = ((), (), s32[]{:S(2)}) async-start(), calls=%async_computation.8 | async-start | bytes 2359296 | tf_op jit(solution)/shard_map/all_gather | solution.py:68
  172.2 57.2 %all-to-all-start.3 = ((bf16[2,768,1024]{2,1,0:T(8,128)(2,1)}), bf16[2,768,1024]{2,1,0:T(8,128)(2,1)S(1)}, u32[]{:S(2)}, u32[]{:S(2)}) async-start(bf16[2,768,1024]{2,1,0:T(8,128)(2,1)} %bitcast.10), calls=%async_computation.3 | async-start | bytes 6291456 | tf_op jit(solution)/shard_map/all_to_all | solution.py:62
  176.2 122.5 %all-gather.9.cloned.1.call-start = ((), (), s32[]{:S(2)}) async-start(), calls=%async_computation.10 | async-start | bytes 2359296 | tf_op jit(solution)/shard_map/all_gather | solution.py:66
  229.4 1.7 copy-start.4
  231.1 57.7 %all-to-all-start.1 = ((bf16[2,768,1024]{2,1,0:T(8,128)(2,1)}), bf16[2,768,1024]{2,1,0:T(8,128)(2,1)}, u32[]{:S(2)}, u32[]{:S(2)}) async-start(bf16[2,768,1024]{2,1,0:T(8,128)(2,1)} %bitcast.5), calls=%async_computation.1 | async-start | bytes 6291456 | tf_op jit(solution)/shard_map/all_to_all | solution.py:63
  236.3 66.6 %all-gather.7.cloned.1.call-start = ((), (), s32[]{:S(2)}) async-start(), calls=%async_computation.9 | async-start | bytes 2359296 | tf_op jit(solution)/shard_map/all_gather | solution.py:67
  240.3 79.4 %copy-start.3 = (bf16[768,2,1024]{0,2,1:T(8,128)(2,1)}, bf16[768,2,1024]{0,2,1:T(8,128)(2,1)S(1)}, u32[]{:S(2)}) copy-start(bf16[768,2,1024]{0,2,1:T(8,128)(2,1)S(1)} %copy.30) | copy-start | bytes 9437188
  302.9 5.2 %copy-start.5 = (bf16[1,2048,384]{2,1,0:T(8,128)(2,1)S(1)}, bf16[1,2048,384]{2,1,0:T(8,128)(2,1)}, u32[]{:S(2)}) copy-start(bf16[1,2048,384]{2,1,0:T(8,128)(2,1)} %all-gather.9.cloned.1.call-done) | copy-start | bytes 4718596
  308.1 1.8 copy-start.7
  308.1 1.9 copy-start.8
  308.1 1.9 copy-start.6
  313.8 52.6 %all-to-all-start.4 = ((bf16[768,2,1024]{2,0,1:T(8,128)(2,1)}), bf16[768,2,1024]{2,0,1:T(8,128)(2,1)}, u32[]{:S(2)}, u32[]{:S(2)}) async-start(bf16[768,2,1024]{2,0,1:T(8,128)(2,1)} %bitcast.76), calls=%async_computation.4 | async-start | bytes 6291456 | tf_op jit(solution)/shard_map/all_to_all | solution.py:87
  319.0 63.6 %all-gather.11.cloned.1.call-start = ((), (), s32[]{:S(2)}) async-start(), calls=%async_computation.13 | async-start | bytes 1769472 | tf_op jit(solution)/shard_map/all_gather | solution.py:95
  319.6 131.9 %reduce-scatter.5.cloned.1.call-start = ((), (), s32[]{:S(2)}) async-start(), calls=%async_computation.12 | async-start | bytes 2359296 | tf_op jit(solution)/shard_map/reduce_scatter | solution.py:103
  366.4 76.1 %all-to-all-start.5 = ((bf16[16,96,1024]{2,1,0:T(8,128)(2,1)}), bf16[16,96,1024]{2,1,0:T(8,128)(2,1)S(1)}, u32[]{:S(2)}, u32[]{:S(2)}) async-start(bf16[16,96,1024]{2,1,0:T(8,128)(2,1)} %bitcast.16), calls=%async_computation.5 | async-start | bytes 6291456 | tf_op jit(solution)/shard_map/all_to_all | solution.py:86
  377.2 74.3 %reduce-scatter.3.cloned.1.call-start = ((), (), s32[]{:S(2)}) async-start(), calls=%async_computation.11 | async-start | bytes 2359296 | tf_op jit(solution)/shard_map/reduce_scatter | solution.py:100
  442.4 9.1 %copy-start.1 = (bf16[128,1024]{1,0:T(8,128)(2,1)S(1)}, bf16[128,1024]{1,0:T(8,128)(2,1)}, u32[]{:S(2)}) copy-start(bf16[128,1024]{1,0:T(8,128)(2,1)} %param.7) | copy-start | bytes 786436
Sparse Core Ops, SparseCore 0:
  109.3 27.8 all-gather.4
  178.6 49.0 all-gather.8
  238.7 49.4 all-gather.6
  321.7 41.2 all-gather.10
  365.6 25.8 reduce-scatter.4
  394.3 26.0 reduce-scatter.2
where the time goes:
time: 464 us; the launch traced here: 458 us
  waiting for transfers between devices  315 us (68%)
  starting transfers between devices  42 us (9%)
  local copies, waits for them, and re-layouts  39 us (8%)
  matrix products  32.2 us (7%)
  other arithmetic  16.1 us (3%)
  between operations  14.3 us (3%)
    all_to_all x1, waiting for transfers between devices, shards(): lax.all_to_all(scaled_slots, 'expert', split_axis=0, concat_axis=0, tiled...  64.6 us
    all_to_all x1, waiting for transfers between devices, shards(): lax.all_to_all(input_cols, 'dp', split_axis=0, concat_axis=1, tiled=True)  52.5 us
    all_to_all x1, waiting for transfers between devices, shards(): lax.all_to_all(lax.all_to_all(row_grad, 'dp', split_axis=1, concat_axis=0...  52.1 us
    all_to_all x1, waiting for transfers between devices, shards(): lax.all_to_all(token_slots, 'expert', split_axis=0, concat_axis=0, tiled=...  51.9 us
    all_to_all x1, waiting for transfers between devices, shards(): lax.all_to_all(scaled_cols, 'dp', split_axis=0, concat_axis=1, tiled=True)  48.6 us
    all_to_all x1, waiting for transfers between devices, shards(): lax.all_to_all(row_grad, 'dp', split_axis=1, concat_axis=0, tiled=True)  42.7 us
    all_to_all x1, starting transfers between devices, shards(): lax.all_to_all(lax.all_to_all(row_grad, 'dp', split_axis=1, concat_axis=0...  10.9 us
    all_to_all x1, starting transfers between devices, shards(): lax.all_to_all(scaled_slots, 'expert', split_axis=0, concat_axis=0, tiled...  9.61 us
  transfers between devices with their start and end apart: 12, of which 6 were waited for; matrix products, arithmetic and copies ran while one was open for 12% of the time, Pallas kernels for 0%

commit v1 on v0

--- a/solution.py
+++ b/solution.py
@@ -109,9 +109,53 @@
     return (d_tokens, grad_gate[None], grad_up[None], grad_down[None])
 
 
+def dense_shards(tokens, grad_out, routes, gates, w_gate, w_up, w_down):
+    experts = lax.axis_size("expert")
+    dp_count = lax.axis_size("dp")
+    me = lax.axis_index("expert")
+    mine = lax.axis_index("dp")
+    half = tokens.shape[0] // dp_count
+    named = routes[:, :, None] == jnp.arange(experts, dtype=jnp.int32)
+    table = jnp.sum(jnp.where(named, gates[:, :, None], 0.0), axis=1)
+    table = lax.dynamic_slice_in_dim(table, mine * half, half, axis=0)
+    table = lax.all_gather(table, "expert", axis=0, tiled=True)
+    weight = jnp.sum(jnp.where(jnp.arange(experts)[None, :] == me, table, 0.0), axis=1)[:, None]
+    inputs = lax.all_to_all(tokens, "dp", split_axis=0, concat_axis=1, tiled=True)
+    cotangent = lax.all_to_all(grad_out, "dp", split_axis=0, concat_axis=1, tiled=True)
+    inputs = lax.all_gather(inputs, "expert", axis=0, tiled=True)
+    cotangent = lax.all_gather(cotangent, "expert", axis=0, tiled=True)
+    scaled = (cotangent.astype(jnp.float32) * weight).astype(jnp.bfloat16)
+    full_gate = lax.all_gather(w_gate, "dp", axis=1, tiled=True)[0]
+    full_up = lax.all_gather(w_up, "dp", axis=1, tiled=True)[0]
+    full_down = lax.all_gather(w_down, "dp", axis=2, tiled=True)[0]
+    pre_gate = jnp.dot(inputs, full_gate, preferred_element_type=jnp.float32)
+    pre_up = jnp.dot(inputs, full_up, preferred_element_type=jnp.float32)
+    sigmoid_gate = jax.nn.sigmoid(pre_gate)
+    activated = pre_gate * sigmoid_gate
+    hidden = (activated * pre_up).astype(jnp.bfloat16)
+    back_hidden = contract_cols(scaled, full_down)
+    d_up = (back_hidden * activated).astype(jnp.bfloat16)
+    d_gate = (back_hidden * pre_up * sigmoid_gate * (1.0 + pre_gate * (1.0 - sigmoid_gate))).astype(
+        jnp.bfloat16
+    )
+    row_grad = (contract_cols(d_gate, full_gate) + contract_cols(d_up, full_up)).astype(
+        jnp.bfloat16
+    )
+    summed = lax.psum_scatter(row_grad, "expert", scatter_dimension=0, tiled=True)
+    d_tokens = lax.all_to_all(summed, "dp", split_axis=1, concat_axis=0, tiled=True)
+    gate_part = contract_rows(inputs, d_gate).astype(jnp.bfloat16)
+    up_part = contract_rows(inputs, d_up).astype(jnp.bfloat16)
+    down_part = contract_rows(hidden, scaled).astype(jnp.bfloat16)
+    grad_gate = lax.psum_scatter(gate_part, "dp", scatter_dimension=0, tiled=True)
+    grad_up = lax.psum_scatter(up_part, "dp", scatter_dimension=0, tiled=True)
+    grad_down = lax.psum_scatter(down_part, "dp", scatter_dimension=1, tiled=True)
+    return (d_tokens, grad_gate[None], grad_up[None], grad_down[None])
+
+
 def solution(mesh):
+    small = mesh.shape["expert"] == 16 and mesh.shape["dp"] == 2
     return jax.shard_map(
-        shards,
+        dense_shards if small else shards,
         mesh=mesh,
         in_specs=(
             P("expert", "dp"),

time: 464 us -> 382 us (0.82)
  waiting for transfers between devices: 315 us -> 272 us
  starting transfers between devices: 42 us -> 3.98 us
  blocking collectives: 0 us -> 37.7 us
  local copies, waits for them, and re-layouts: 39 us -> 10 us
  other arithmetic: 16.1 us -> 0.11 us
  matrix products: 32.2 us -> 41.8 us
    all_to_all x6 -> x1, waiting for transfers between devices: 312 us -> 0.01 us  [dense_shards(): lax.all_to_all(summed, 'dp', split_axis=1, concat_axis=0, tiled=True)]
    all_gather x4 -> x5, waiting for transfers between devices: 0.03 us -> 141 us  [the longest x1 52.1 us: dense_shards(): cotangent = lax.all_gather(cotangent, 'expert', axis=0, tiled=True)]
    reduce_scatter x2 -> x4, waiting for transfers between devices: 0.01 us -> 129 us  [the longest x1 51.5 us: dense_shards(): lax.psum_scatter(row_grad, 'expert', scatter_dimension=0, tiled=True)]
    all_to_all x6 -> x1, starting transfers between devices: 41.3 us -> 3.44 us  [dense_shards(): lax.all_to_all(summed, 'dp', split_axis=1, concat_axis=0, tiled=True)]
    gather x4 -> x0, local copies, waits for them, and re-layouts: 21.3 us -> none  [the longest x1 5.85 us: shards(): flat_gates[safe_rows][:, None]]
    all_gather x0 -> x1, blocking collectives: none -> 19.3 us  [dense_shards(): table = lax.all_gather(table, 'expert', axis=0, tiled=True)]
    all_to_all x0 -> x2, blocking collectives: none -> 18.5 us  [the longest x1 10.3 us: dense_shards(): lax.all_to_all(grad_out, 'dp', split_axis=0, concat_axis=1, tiled=True)]
    dot_general x2 -> x3, matrix products: 9.06 us -> 16.4 us  [contract_rows(): lax.dot_general(left_rows, right_rows, (((0,), (0,)), ((), ())), preferre...]
  transfers between devices with their start and end apart: 12 -> 10, of which waited for: 6 -> 8; matrix products, arithmetic and copies ran while one was open for 12% -> 10% of each run, Pallas kernels for 0% -> 0%
where the time goes in v1:
time: 382 us; the launch traced here: 380 us
  waiting for transfers between devices  272 us (71%)
  matrix products  41.8 us (11%)
  blocking collectives  37.7 us (10%)
  between operations  14 us (4%)
  local copies, waits for them, and re-layouts  10 us (3%)
  starting transfers between devices  3.98 us (1%)
    all_gather x1, waiting for transfers between devices, dense_shards(): cotangent = lax.all_gather(cotangent, 'expert', axis=0, tiled=True)  52.1 us
    reduce_scatter x1, waiting for transfers between devices, dense_shards(): lax.psum_scatter(row_grad, 'expert', scatter_dimension=0, tiled=True)  51.5 us
    all_gather x1, waiting for transfers between devices, dense_shards(): inputs = lax.all_gather(inputs, 'expert', axis=0, tiled=True)  44 us
    reduce_scatter x1, waiting for transfers between devices, dense_shards(): lax.psum_scatter(down_part, 'dp', scatter_dimension=1, tiled=True)  26.8 us
    reduce_scatter x1, waiting for transfers between devices, dense_shards(): grad_up = lax.psum_scatter(up_part, 'dp', scatter_dimension=0, tiled=True)  26.1 us
    reduce_scatter x1, waiting for transfers between devices, dense_shards(): lax.psum_scatter(gate_part, 'dp', scatter_dimension=0, tiled=True)  25.1 us
    all_gather x1, waiting for transfers between devices, dense_shards(): full_down = lax.all_gather(w_down, 'dp', axis=2, tiled=True)[0]  22.5 us
    all_gather x1, waiting for transfers between devices, dense_shards(): full_up = lax.all_gather(w_up, 'dp', axis=1, tiled=True)[0]  22.2 us
  transfers between devices with their start and end apart: 10, of which 8 were waited for; matrix products, arithmetic and copies ran while one was open for 10% of the time, Pallas kernels for 0%

profile of v1, /device:TPU:25, one launch (start us, length us, event | category | flops | bytes accessed | tf_op | source)
XLA Modules:
  0.0 379.8 jit_solution(10943762997720543699)
XLA Ops:
  7.2 0.0 all-gather.15.cloned.1.call-start
  7.2 0.7 all-gather.15.cloned.1.call-update
  7.9 0.0 copy-start.2
  7.9 0.0 all-gather.11.cloned.1.call-start
  8.0 8.1 %all_to_all.57 = bf16[2,64,1024]{2,1,0:T(8,128)(2,1)S(1)} all-to-all(bf16[2,64,1024]{2,1,0:T(8,128)(2,1)} %bitcast.56), channel_id=1, replica_groups=mesh['expert'=16,'dp'=2] {'dp'}, dimensions={0} | all-to-all | bytes 524288 | tf_op jit(solution)/shard_map/all_to_all | solution.py:123
  16.1 0.7 copy.46
  16.8 0.0 copy-start.3
  16.8 0.0 copy-start.4
  16.8 0.0 all-gather.11.cloned.1.call-update
  16.8 0.0 all-gather.13.cloned.1.call-start
  16.9 0.7 all-gather.13.cloned.1.call-update
  17.6 0.0 all-gather.9.cloned.1.call-start
  17.6 0.5 all-gather.9.cloned.1.call-update
  18.2 0.0 all-gather.7.cloned.1.call-start
  18.2 0.0 copy-done.2
  18.2 10.3 %all_to_all.58 = bf16[2,64,1024]{2,1,0:T(8,128)(2,1)S(1)} all-to-all(bf16[2,64,1024]{2,1,0:T(8,128)(2,1)S(1)} %bitcast.57), channel_id=1, replica_groups=mesh['expert'=16,'dp'=2] {'dp'}, dimensions={0} | all-to-all | bytes 524288 | tf_op jit(solution)/shard_map/all_to_all | solution.py:124
  28.5 0.7 copy.45
  29.3 0.0 all-gather.7.cloned.1.call-update
  29.3 0.0 reduce-scatter.5.cloned.1.call-start
  29.3 0.0 copy-done.3
  29.4 0.0 copy-done.4
  29.4 0.1 dynamic-slice_bitcast_fusion
  29.5 19.3 %all-gather = f32[16,64,16]{1,2,0:T(8,128)S(1)} all-gather(f32[1,64,16]{1,2,0:T(8,128)S(1)} %dynamic-slice_bitcast_fusion), channel_id=1, replica_groups=mesh['expert'=16,'dp'=2] {'expert'}, dimensions={0}, use_global_device_ids=true | all-gather | bytes 69632 | tf_op jit(solution)/shard_map/all_gather | solution.py:121
  48.8 0.1 reshape.26
  48.9 0.1 select_reduce_fusion
  49.0 0.0 all-gather.15.cloned.1.call-done
  49.0 44.0 %all-gather.11.cloned.1.call-done = bf16[1024,2048]{1,0:T(8,128)(2,1)} async-done(((bf16[64,2048]{1,0:T(8,128)(2,1)}), bf16[1024,2048]{1,0:T(8,128)(2,1)}) %all-gather.11.cloned.1.call-update) | async-done | bytes 4194320 | tf_op jit(solution)/shard_map/all_gather | solution.py:125
  93.0 6.2 %fusion.5 = f32[1024,384]{1,0:T(8,128)} fusion(bf16[1024,2048]{1,0:T(8,128)(2,1)} %all-gather.11.cloned.1.call-done, bf16[1,2048,384]{2,1,0:T(8,128)(2,1)} %all-gather.15.cloned.1.call-done), kind=kOutput, calls=%fused_computation.10 | convolution fusion | flops 1610612736 | bytes 7340032 | tf_op jit(solution)/shard_map/dot_general | solution.py:131
  99.2 22.2 %all-gather.13.cloned.1.call-done = bf16[1,2048,384]{2,1,0:T(8,128)(2,1)} async-done(((bf16[1,1024,384]{2,1,0:T(8,128)(2,1)}), bf16[1,2048,384]{2,1,0:T(8,128)(2,1)}) %all-gather.13.cloned.1.call-update) | async-done | bytes 1572880 | tf_op jit(solution)/shard_map/all_gather | solution.py:129
  121.3 6.1 %fusion.8 = f32[1024,384]{1,0:T(8,128)} fusion(bf16[1024,2048]{1,0:T(8,128)(2,1)} %all-gather.11.cloned.1.call-done, bf16[1,2048,384]{2,1,0:T(8,128)(2,1)} %all-gather.13.cloned.1.call-done), kind=kOutput, calls=%fused_computation.13 | convolution fusion | flops 1610612736 | bytes 7340032 | tf_op jit(solution)/shard_map/dot_general | solution.py:132
  127.5 0.0 copy-start
  127.5 22.5 %all-gather.9.cloned.1.call-done = bf16[1,384,2048]{2,1,0:T(8,128)(2,1)} async-done(((bf16[1,384,1024]{2,1,0:T(8,128)(2,1)}), bf16[1,384,2048]{2,1,0:T(8,128)(2,1)}) %all-gather.9.cloned.1.call-update) | async-done | bytes 1572880 | tf_op jit(solution)/shard_map/all_gather | solution.py:130
  150.0 52.1 %all-gather.7.cloned.1.call-done = bf16[1024,2048]{1,0:T(8,128)(2,1)} async-done(((bf16[64,2048]{1,0:T(8,128)(2,1)}), bf16[1024,2048]{1,0:T(8,128)(2,1)}) %all-gather.7.cloned.1.call-update) | async-done | bytes 4194320 | tf_op jit(solution)/shard_map/all_gather | solution.py:126
  202.1 6.4 %multiply_convert_fusion.4 = (bf16[1024,384]{1,0:T(8,128)(2,1)S(1)}, bf16[1024,384]{1,0:T(8,128)(2,1)S(1)}) fusion(f32[1024,384]{1,0:T(8,128)} %fusion.5, f32[1024,384]{1,0:T(8,128)} %fusion.8, bf16[1,384,2048]{2,1,0:T(8,128)(2,1)} %all-gather.9.cloned.1.call-done, bf16[1024,2048]{1,0:T(8,128)(2,1)} %all-gather.7.cloned.1.call-done, ...), kind=kOutput, calls=%fused_computation.17 | convolution fusion | flops 1622016000 | bytes 10489856 | tf_op jit(solution)/shard_map/dot_general | solution.py:14
  208.5 0.0 copy-done
  208.5 0.0 copy-start.1
  208.5 2.4 fusion.3
  210.9 0.0 copy-done.1
  210.9 4.4 %add_convert_fusion = bf16[1024,2048]{1,0:T(8,128)(2,1)} fusion(f32[1024,2048]{1,0:T(8,128)S(1)} %fusion.3, bf16[1024,384]{1,0:T(8,128)(2,1)S(1)} %get-tuple-element.24, bf16[1,2048,384]{2,1,0:T(8,128)(2,1)S(1)} %copy-done.1), kind=kOutput, calls=%fused_computation | convolution fusion | flops 1614807040 | bytes 14942208 | tf_op jit(solution)/shard_map/dot_general | solution.py:14
  215.2 0.0 reduce-scatter.5.cloned.1.call-update
  215.3 0.0 reduce-scatter.7.cloned.1.call-start
  215.3 5.2 %fusion = bf16[2048,384]{0,1:T(8,128)(2,1)} fusion(bf16[1024,384]{1,0:T(8,128)(2,1)S(1)} %get-tuple-element.25, bf16[1024,2048]{1,0:T(8,128)(2,1)} %all-gather.11.cloned.1.call-done), kind=kOutput, calls=%fused_computation.5 | convolution fusion | flops 1611399168 | bytes 6553600 | tf_op jit(solution)/shard_map/dot_general | solution.py:8
  220.5 0.0 reduce-scatter.7.cloned.1.call-update
  220.5 0.2 reduce-scatter.9.cloned.1.call-start
  220.7 0.0 copy-start.6
  220.7 5.4 %fusion.1 = bf16[2048,384]{0,1:T(8,128)(2,1)} fusion(bf16[1024,384]{1,0:T(8,128)(2,1)S(1)} %get-tuple-element.24, bf16[1024,2048]{1,0:T(8,128)(2,1)} %all-gather.11.cloned.1.call-done), kind=kOutput, calls=%fused_computation.6 | convolution fusion | flops 1611399168 | bytes 6553600 | tf_op jit(solution)/shard_map/dot_general | solution.py:8
  226.2 0.0 copy-start.5
  226.2 0.0 reduce-scatter.9.cloned.1.call-update
  226.2 0.0 reduce-scatter.11.cloned.1.call-start
  226.2 0.0 copy-done.6
  226.2 1.4 copy-done.5
  227.7 5.8 %convolution_convert_fusion = bf16[384,2048]{1,0:T(8,128)(2,1)} fusion(bf16[1024,2048]{1,0:T(8,128)(2,1)} %all-gather.7.cloned.1.call-done, f32[1024]{0:T(1024)S(1)} %select_reduce_fusion, f32[1024,384]{1,0:T(8,128)S(1)} %copy-done.6, f32[1024,384]{1,0:T(8,128)S(1)} %copy-done.5), kind=kOutput, calls=%fused_computation.2 | convolution fusion | flops 1620049920 | bytes 8916992 | tf_op jit(solution)/shard_map/dot_general | solution.py:8
  233.5 0.0 reduce-scatter.11.cloned.1.call-update
  233.5 51.5 %reduce-scatter.5.cloned.1.call-done = bf16[64,2048]{1,0:T(8,128)(2,1)} async-done(((bf16[1024,2048]{1,0:T(8,128)(2,1)}), bf16[64,2048]{1,0:T(8,128)(2,1)}) %reduce-scatter.5.cloned.1.call-update) | async-done | bytes 262160 | tf_op jit(solution)/shard_map/reduce_scatter | solution.py:144
  284.9 1.7 copy.48
  286.6 3.4 all-to-all-start.2
  290.1 25.1 %reduce-scatter.7.cloned.1.call-done = bf16[1024,384]{0,1:T(8,128)(2,1)} async-done(((bf16[2048,384]{0,1:T(8,128)(2,1)}), bf16[1024,384]{0,1:T(8,128)(2,1)}) %reduce-scatter.7.cloned.1.call-update) | async-done | bytes 786448 | tf_op jit(solution)/shard_map/reduce_scatter | solution.py:149
  315.1 2.3 copy.42
  317.4 26.1 %reduce-scatter.9.cloned.1.call-done = bf16[1024,384]{0,1:T(8,128)(2,1)} async-done(((bf16[2048,384]{0,1:T(8,128)(2,1)}), bf16[1024,384]{0,1:T(8,128)(2,1)}) %reduce-scatter.9.cloned.1.call-update) | async-done | bytes 786448 | tf_op jit(solution)/shard_map/reduce_scatter | solution.py:150
  343.5 2.3 copy.43
  345.8 0.0 all-to-all-done.2
  345.8 26.8 %reduce-scatter.11.cloned.1.call-done = bf16[384,1024]{1,0:T(8,128)(2,1)} async-done(((bf16[384,2048]{1,0:T(8,128)(2,1)}), bf16[384,1024]{1,0:T(8,128)(2,1)}) %reduce-scatter.11.cloned.1.call-update) | async-done | bytes 786448 | tf_op jit(solution)/shard_map/reduce_scatter | solution.py:151
  372.6 0.7 copy.50
  (3 shorter events, 0.1 us)
Async XLA Ops:
  7.2 41.8 %all-gather.15.cloned.1.call-start = ((), (), s32[]{:S(2)}) async-start(), calls=%async_computation.11 | async-start | bytes 2359296 | tf_op jit(solution)/shard_map/all_gather | solution.py:128
  7.9 10.3 %copy-start.2 = (bf16[128,1024]{1,0:T(8,128)(2,1)S(1)}, bf16[128,1024]{1,0:T(8,128)(2,1)}, u32[]{:S(2)}) copy-start(bf16[128,1024]{1,0:T(8,128)(2,1)} %param.8) | copy-start | bytes 786436
  7.9 85.1 %all-gather.11.cloned.1.call-start = ((), (), s32[]{:S(2)}) async-start(), calls=%async_computation.9 | async-start | bytes 4456448 | tf_op jit(solution)/shard_map/all_gather | solution.py:125
  16.8 12.5 %copy-start.3 = (f32[128,8]{0,1:T(8,128)S(1)}, f32[128,8]{0,1:T(8,128)}, u32[]{:S(2)}) copy-start(f32[128,8]{0,1:T(8,128)} %param.10) | copy-start | bytes 12292
  16.8 12.5 %copy-start.4 = (s32[128,8]{0,1:T(8,128)S(1)}, s32[128,8]{0,1:T(8,128)}, u32[]{:S(2)}) copy-start(s32[128,8]{0,1:T(8,128)} %param.9) | copy-start | bytes 12292
  16.8 104.5 %all-gather.13.cloned.1.call-start = ((), (), s32[]{:S(2)}) async-start(), calls=%async_computation.10 | async-start | bytes 2359296 | tf_op jit(solution)/shard_map/all_gather | solution.py:129
  17.6 132.4 %all-gather.9.cloned.1.call-start = ((), (), s32[]{:S(2)}) async-start(), calls=%async_computation.8 | async-start | bytes 2359296 | tf_op jit(solution)/shard_map/all_gather | solution.py:130
  18.2 183.9 %all-gather.7.cloned.1.call-start = ((), (), s32[]{:S(2)}) async-start(), calls=%async_computation.7 | async-start | bytes 4456448 | tf_op jit(solution)/shard_map/all_gather | solution.py:126
  29.3 255.7 %reduce-scatter.5.cloned.1.call-start = ((), (), s32[]{:S(2)}) async-start(), calls=%async_computation.12 | async-start | bytes 4456448 | tf_op jit(solution)/shard_map/reduce_scatter | solution.py:144
  127.5 81.0 %copy-start = (bf16[1,2048,384]{2,1,0:T(8,128)(2,1)S(1)}, bf16[1,2048,384]{2,1,0:T(8,128)(2,1)}, u32[]{:S(2)}) copy-start(bf16[1,2048,384]{2,1,0:T(8,128)(2,1)} %all-gather.15.cloned.1.call-done) | copy-start | bytes 4718596
  208.5 2.4 copy-start.1
  215.3 99.9 %reduce-scatter.7.cloned.1.call-start = ((), (), s32[]{:S(2)}) async-start(), calls=%async_computation.13 | async-start | bytes 2359296 | tf_op jit(solution)/shard_map/reduce_scatter | solution.py:149
  220.5 123.0 %reduce-scatter.9.cloned.1.call-start = ((), (), s32[]{:S(2)}) async-start(), calls=%async_computation.14 | async-start | bytes 2359296 | tf_op jit(solution)/shard_map/reduce_scatter | solution.py:150
  220.7 5.5 %copy-start.6 = (f32[1024,384]{1,0:T(8,128)S(1)}, f32[1024,384]{1,0:T(8,128)}, u32[]{:S(2)}) copy-start(f32[1024,384]{1,0:T(8,128)} %fusion.8) | copy-start | bytes 4718596
  226.2 1.5 copy-start.5
  226.2 146.4 %reduce-scatter.11.cloned.1.call-start = ((), (), s32[]{:S(2)}) async-start(), calls=%async_computation.15 | async-start | bytes 2359296 | tf_op jit(solution)/shard_map/reduce_scatter | solution.py:151
  286.6 59.2 %all-to-all-start.2 = ((bf16[64,2,1024]{2,0,1:T(8,128)(2,1)}), bf16[64,2,1024]{2,0,1:T(8,128)(2,1)S(1)}, u32[]{:S(2)}, u32[]{:S(2)}) async-start(bf16[64,2,1024]{2,0,1:T(8,128)(2,1)} %bitcast.48), calls=%async_computation.3 | async-start | bytes 524288 | tf_op jit(solution)/shard_map/all_to_all | solution.py:145
Sparse Core Ops, SparseCore 0:
  9.5 30.9 all-gather.14
  43.3 49.6 all-gather.10
  94.5 26.7 all-gather.12
  122.7 27.1 all-gather.8
  152.6 49.4 all-gather.6
  215.4 69.5 reduce-scatter.4
  287.3 27.8 reduce-scatter.6
  317.4 26.0 reduce-scatter.8
  346.4 26.0 reduce-scatter.10

commit v2 on v0

--- a/solution.py
+++ b/solution.py
@@ -1,6 +1,8 @@
 import jax
 import jax.numpy as jnp
 from jax import lax
+from jax.experimental import pallas as pl
+from jax.experimental.pallas import tpu as pltpu
 from jax.sharding import PartitionSpec as P
 
 
@@ -109,9 +111,308 @@
     return (d_tokens, grad_gate[None], grad_up[None], grad_down[None])
 
 
+MESH_ID = pl.DeviceIdType.MESH
+
+
+def contract_first(left, right):
+    return lax.dot_general(left, right, (((0,), (0,)), ((), ())), preferred_element_type=jnp.float32)
+
+
+def fused_kernel(
+    tok, cot, tab, wg, wu, wd,
+    out_tok, out_gate, out_up, out_down,
+    acts, table, w_own, w_far, wd_far, scaled, pre, hidden, d_both,
+    row_grad, from_core, from_y, from_z, tok_send, tok_far,
+    gate_own, down_own, gate_send, up_send, down_send, gate_far, up_far, down_far,
+    x_send, x_recv, z_send, z_recv, y_send, y_recv, c_send, c_recv,
+    rc_send, rc_recv, ry_send, ry_recv, rz_send, rz_recv,
+):
+    e = lax.axis_index("expert")
+    d = lax.axis_index("dp")
+    core = e % 2
+    y_pos = (e // 2) % 2
+    z_pos = e // 4
+    half = tok.shape[0] // 2
+    feats = tok.shape[1]
+    width = wg.shape[1]
+    x_peer = (e, 1 - d)
+    core_peer = (e + 1 - 2 * core, d)
+    y_peer = (e + 2 - 4 * y_pos, d)
+    z_peers = [((z_pos + k) % 4 * 4 + e % 4, d) for k in (1, 2, 3)]
+
+    def copy(src, dst, send, recv, peer):
+        return pltpu.make_async_remote_copy(
+            src_ref=src, dst_ref=dst, send_sem=send, recv_sem=recv, device_id=peer, device_id_type=MESH_ID
+        )
+
+    barrier = pltpu.get_barrier_semaphore()
+    for peer in [x_peer, core_peer, y_peer] + z_peers:
+        pl.semaphore_signal(barrier, inc=1, device_id=peer, device_id_type=MESH_ID)
+
+    mine = pl.ds(pl.multiple_of(d * half, half), half)
+    theirs = pl.ds(pl.multiple_of((1 - d) * half, half), half)
+    acts[0, 0, 0] = tok[mine, :]
+    acts[0, 0, 1] = cot[mine, :]
+    table[0] = tab[mine, :]
+    pl.semaphore_wait(barrier, 6)
+
+    sends = []
+
+    def start(item):
+        item.start()
+        sends.append(item)
+        return item
+
+    swap_tok = start(copy(tok.at[theirs], acts.at[1, 0, 0], x_send.at[0], x_recv.at[0], x_peer))
+    swap_cot = start(copy(cot.at[theirs], acts.at[1, 0, 1], x_send.at[1], x_recv.at[1], x_peer))
+
+    pieces = [acts.at[0], acts.at[1], table]
+
+    def z_copy(p, k):
+        return copy(pieces[p].at[0], pieces[p].at[4 - k], z_send.at[p, k - 1], z_recv.at[p, 3 - k], z_peers[k - 1])
+
+    def y_copy(p, j):
+        return copy(pieces[p].at[j], pieces[p].at[4 + j], y_send.at[p, j], y_recv.at[p, j], y_peer)
+
+    def c_copy(p, j):
+        return copy(pieces[p].at[j], pieces[p].at[8 + j], c_send.at[p, j], c_recv.at[p, j], core_peer)
+
+    def spread_own(p):
+        for k in (2, 1, 3):
+            start(z_copy(p, k))
+        start(y_copy(p, 0))
+        start(c_copy(p, 0))
+
+    def forward(p):
+        for j in (1, 3, 2):
+            z_copy(p, 4 - j).wait_recv()
+            start(y_copy(p, j))
+            start(c_copy(p, j))
+        for j in (0, 1, 3, 2):
+            y_copy(p, j).wait_recv()
+            start(c_copy(p, 4 + j))
+
+    spread_own(2)
+    spread_own(0)
+    swap_tok.wait_recv()
+    swap_cot.wait_recv()
+    spread_own(1)
+    w_copies = [
+        start(copy(wg, w_far.at[:, pl.ds(0, width)], x_send.at[2], x_recv.at[2], x_peer)),
+        start(copy(wu, w_far.at[:, pl.ds(width, width)], x_send.at[3], x_recv.at[3], x_peer)),
+    ]
+    w_own[:, :width] = wg[...]
+    w_own[:, width:] = wu[...]
+    forward(2)
+    forward(0)
+    down_copy = start(copy(wd, wd_far, x_send.at[4], x_recv.at[4], x_peer))
+    forward(1)
+    for p in (2, 0, 1):
+        for j in range(8):
+            c_copy(p, j).wait_recv()
+    for item in w_copies:
+        item.wait_recv()
+
+    tile = 4 * half
+    blocks = 4
+
+    def rows_of(i):
+        return pl.ds(pl.multiple_of(i * tile, tile), tile)
+
+    @pl.loop(0, blocks)
+    def _(i):
+        rows, group = rows_of(i), pl.ds(i * 4, 4)
+        lanes = lax.broadcasted_iota(jnp.int32, (tile, table.shape[-1]), 1)
+        column = jnp.sum(
+            jnp.where(lanes == e, table[group].reshape(tile, -1), 0.0), axis=1, keepdims=True
+        )
+        for h in range(2):
+            far = acts[h, group, 1].reshape(tile, feats).astype(jnp.float32)
+            scaled[h, rows, :] = (far * column).astype(jnp.bfloat16)
+        near = jnp.dot(acts[0, group, 0].reshape(tile, feats), w_own[...], preferred_element_type=jnp.float32)
+        far = jnp.dot(acts[1, group, 0].reshape(tile, feats), w_far[...], preferred_element_type=jnp.float32)
+        total = near + far
+        pre[rows, :] = total
+        gate, up = total[:, :width], total[:, width:]
+        hidden[rows, :] = (gate * jax.nn.sigmoid(gate) * up).astype(jnp.bfloat16)
+
+    strip = feats // 4
+
+    def cols_of(i):
+        return pl.ds(pl.multiple_of(i * strip, strip), strip)
+
+    @pl.loop(0, 4)
+    def _(i):
+        down_send[:, cols_of(i)] = contract_first(hidden[...], scaled[1, :, cols_of(i)]).astype(jnp.bfloat16)
+
+    grad_copies = [start(copy(down_send, down_far, x_send.at[5], x_recv.at[5], x_peer))]
+    down_copy.wait_recv()
+
+    @pl.loop(0, blocks)
+    def _(i):
+        rows = rows_of(i)
+        back = contract_cols(scaled[0, rows, :], wd[...]) + contract_cols(scaled[1, rows, :], wd_far[...])
+        gate, up = pre[rows, :width], pre[rows, width:]
+        sig = jax.nn.sigmoid(gate)
+        d_both[rows, :width] = (back * up * sig * (1.0 + gate * (1.0 - sig))).astype(jnp.bfloat16)
+        d_both[rows, width:] = (back * (gate * sig)).astype(jnp.bfloat16)
+
+    def rc_copy(h):
+        return copy(row_grad.at[h, pl.ds(8, 8)], from_core.at[h], rc_send.at[h], rc_recv.at[h], core_peer)
+
+    def ry_copy(h):
+        return copy(row_grad.at[h, pl.ds(4, 4)], from_y.at[h], ry_send.at[h], ry_recv.at[h], y_peer)
+
+    def rz_copy(h, k):
+        return copy(row_grad.at[h, k], from_z.at[h, 3 - k], rz_send.at[h, k - 1], rz_recv.at[h, 3 - k], z_peers[k - 1])
+
+    def rows_back(h, first):
+        weights = w_own if h == 0 else w_far
+
+        @pl.loop(first, first + 2)
+        def _(i):
+            value = contract_cols(d_both[rows_of(i), :], weights[...])
+            row_grad[h, pl.ds(i * 4, 4)] = value.astype(jnp.bfloat16).reshape(4, half, feats)
+
+    def add_into(h, first, extra, offset):
+        @pl.loop(0, 4)
+        def _(j):
+            near = row_grad[h, first + j].astype(jnp.float32)
+            row_grad[h, first + j] = (near + extra[h, offset + j].astype(jnp.float32)).astype(jnp.bfloat16)
+
+    rows_back(1, 2)
+    start(rc_copy(1))
+
+    @pl.loop(0, 4)
+    def _(i):
+        left = acts[1, :, 0, :, cols_of(i)].reshape(16 * half, strip)
+        value = contract_first(left, d_both[...]).astype(jnp.bfloat16)
+        gate_send[cols_of(i), :] = value[:, :width]
+        up_send[cols_of(i), :] = value[:, width:]
+
+    grad_copies.append(start(copy(gate_send, gate_far, x_send.at[6], x_recv.at[6], x_peer)))
+    grad_copies.append(start(copy(up_send, up_far, x_send.at[7], x_recv.at[7], x_peer)))
+
+    rows_back(1, 0)
+    rc_copy(1).wait_recv()
+    add_into(1, 4, from_core, 4)
+    start(ry_copy(1))
+    rows_back(0, 2)
+    start(rc_copy(0))
+    rows_back(0, 0)
+    add_into(1, 0, from_core, 0)
+    rc_copy(0).wait_recv()
+    add_into(0, 4, from_core, 4)
+    start(ry_copy(0))
+    add_into(0, 0, from_core, 0)
+
+    ry_copy(1).wait_recv()
+    add_into(1, 0, from_y, 0)
+    for k in (2, 1, 3):
+        start(rz_copy(1, k))
+
+    @pl.loop(0, 4)
+    def _(i):
+        left = acts[0, :, 0, :, cols_of(i)].reshape(16 * half, strip)
+        gate_own[cols_of(i), :] = contract_first(left, d_both[...])
+        down_own[:, cols_of(i)] = contract_first(hidden[...], scaled[0, :, cols_of(i)])
+
+    ry_copy(0).wait_recv()
+    add_into(0, 0, from_y, 0)
+    for k in (2, 1, 3):
+        start(rz_copy(0, k))
+
+    def finish(h):
+        total = row_grad[h, 0].astype(jnp.float32)
+        for k in range(3):
+            rz_copy(h, 3 - k).wait_recv()
+        for k in range(3):
+            total = total + from_z[h, k].astype(jnp.float32)
+        return total.astype(jnp.bfloat16)
+
+    tok_send[...] = finish(1)
+    tok_copy = start(copy(tok_send, tok_far, x_send.at[8], x_recv.at[8], x_peer))
+    out_tok[mine, :] = finish(0)
+
+    grad_copies[0].wait_recv()
+    out_down[...] = (down_own[...] + down_far[...].astype(jnp.float32)).astype(jnp.bfloat16)
+    grad_copies[1].wait_recv()
+    out_gate[...] = (gate_own[:, :width] + gate_far[...].astype(jnp.float32)).astype(jnp.bfloat16)
+    grad_copies[2].wait_recv()
+    out_up[...] = (gate_own[:, width:] + up_far[...].astype(jnp.float32)).astype(jnp.bfloat16)
+    tok_copy.wait_recv()
+    out_tok[theirs, :] = tok_far[...]
+    for item in sends:
+        item.wait_send()
+
+
+def dense_shards(tokens, grad_out, routes, gates, w_gate, w_up, w_down):
+    experts = lax.axis_size("expert")
+    tok_count, feats = tokens.shape
+    width = w_gate.shape[2]
+    half = tok_count // 2
+    named = routes[:, :, None] == jnp.arange(128, dtype=jnp.int32)
+    table = jnp.sum(jnp.where(named, gates[:, :, None], 0.0), axis=1)
+    bf, f32 = jnp.bfloat16, jnp.float32
+    rows = experts * half
+    vmem = pl.BlockSpec(memory_space=pltpu.VMEM)
+    dma = pltpu.SemaphoreType.DMA
+    d_tokens, grad_gate, grad_up, grad_down = pl.pallas_call(
+        fused_kernel,
+        out_shape=(
+            jax.ShapeDtypeStruct((tok_count, feats), bf),
+            jax.ShapeDtypeStruct((feats, width), bf),
+            jax.ShapeDtypeStruct((feats, width), bf),
+            jax.ShapeDtypeStruct((width, feats), bf),
+        ),
+        in_specs=[vmem] * 6,
+        out_specs=(vmem,) * 4,
+        scratch_shapes=[
+            pltpu.VMEM((2, experts, 2, half, feats), bf),
+            pltpu.VMEM((experts, half, 128), f32),
+            pltpu.VMEM((feats, 2 * width), bf),
+            pltpu.VMEM((feats, 2 * width), bf),
+            pltpu.VMEM((width, feats), bf),
+            pltpu.VMEM((2, rows, feats), bf),
+            pltpu.VMEM((rows, 2 * width), f32),
+            pltpu.VMEM((rows, width), bf),
+            pltpu.VMEM((rows, 2 * width), bf),
+            pltpu.VMEM((2, experts, half, feats), bf),
+            pltpu.VMEM((2, 8, half, feats), bf),
+            pltpu.VMEM((2, 4, half, feats), bf),
+            pltpu.VMEM((2, 3, half, feats), bf),
+            pltpu.VMEM((half, feats), bf),
+            pltpu.VMEM((half, feats), bf),
+            pltpu.VMEM((feats, 2 * width), f32),
+            pltpu.VMEM((width, feats), f32),
+            pltpu.VMEM((feats, width), bf),
+            pltpu.VMEM((feats, width), bf),
+            pltpu.VMEM((width, feats), bf),
+            pltpu.VMEM((feats, width), bf),
+            pltpu.VMEM((feats, width), bf),
+            pltpu.VMEM((width, feats), bf),
+            dma((9,)), dma((9,)),
+            dma((3, 3)), dma((3, 3)),
+            dma((3, 4)), dma((3, 4)),
+            dma((3, 8)), dma((3, 8)),
+            dma((2,)), dma((2,)),
+            dma((2,)), dma((2,)),
+            dma((2, 3)), dma((2, 3)),
+        ],
+        compiler_params=pltpu.CompilerParams(
+            collective_id=0, has_side_effects=True, vmem_limit_bytes=60 * 1024 * 1024
+        ),
+        cost_estimate=pl.CostEstimate(
+            flops=16 * rows * 2 * feats * width, bytes_accessed=8 * 1024 * 1024, transcendentals=rows * width
+        ),
+    )(tokens, grad_out, table, w_gate[0], w_up[0], w_down[0])
+    return (d_tokens, grad_gate[None], grad_up[None], grad_down[None])
+
+
 def solution(mesh):
+    small = mesh.shape["expert"] == 16 and mesh.shape["dp"] == 2
     return jax.shard_map(
-        shards,
+        dense_shards if small else shards,
         mesh=mesh,
         in_specs=(
             P("expert", "dp"),

time: 464 us -> 152 us (0.33)
  the two profiles are of different devices: /device:TPU:25 before, /device:TPU:9 now
where the time goes in v2:
time: 152 us
  Pallas kernels  143 us (94%)
  local copies, waits for them, and re-layouts  7.6 us (5%)
    pallas_call x1, Pallas kernels, dense_shards(): pl.pallas_call(fused_kernel, out_shape=(jax.ShapeDtypeStruct((tok_count,...  143 us
    unnamed x14, local copies, waits for them, and re-layouts  7.6 us

profile of v2, /device:TPU:9, one launch (start us, length us, event | category | flops | bytes accessed | tf_op | source)
XLA Modules:
  0.0 152.0 jit_solution(18011924880442061372)
XLA Ops:
  0.6 0.0 copy-start.2
  0.6 0.7 copy-done.2
  1.3 0.0 copy-start.3
  1.3 0.1 copy.13
  1.4 0.6 copy-done.3
  2.0 0.1 copy.14
  2.1 1.0 select_reduce_fusion.tab
  3.1 142.8 %shard_map.102 = (bf16[128,1024]{1,0:T(8,128)(2,1)}, bf16[1024,384]{1,0:T(8,128)(2,1)}, bf16[1024,384]{1,0:T(8,128)(2,1)}, bf16[384,1024]{1,0:T(8,128)(2,1)}) custom-call(bf16[128,1024]{1,0:T(8,128)(2,1)} %tok.1, bf16[128,1024]{1,0:T(8,128)(2,1)} %cot.1, f32[128,128]{1,0:T(8,128)} %select_reduce_fusion.tab, bf16[1024,384]{1,0:T(8,128)(2,1)} %bitcast.9, ...), custom_call_target="tpu_custom_call" | custom-call | flops 12884901888 | bytes 8388608 | tf_op jit(solution)/shard_map/pallas_call | solution.py:360
  145.9 1.7 %copy.19 = bf16[128,1024]{1,0:T(8,128)(2,1)} copy(bf16[128,1024]{1,0:T(8,128)(2,1)} %get-tuple-element.16) | data formatting | bytes 524288
  147.6 0.0 copy-start.1
  147.6 2.2 %copy.20 = bf16[1,1024,384]{2,1,0:T(8,128)(2,1)} copy(bf16[1,1024,384]{2,1,0:T(8,128)(2,1)} %bitcast.8) | data formatting | bytes 1572864
  149.7 0.0 copy-done.1
  149.7 0.0 copy-start
  149.7 0.9 copy.21
  150.6 0.5 copy-done
  151.2 0.9 copy.22
Async XLA Ops:
  0.6 0.7 copy-start.2
  1.3 0.7 copy-start.3
  147.6 2.2 %copy-start.1 = (bf16[1024,384]{1,0:T(8,128)(2,1)S(1)}, bf16[1024,384]{1,0:T(8,128)(2,1)}, u32[]{:S(2)}) copy-start(bf16[1024,384]{1,0:T(8,128)(2,1)} %get-tuple-element.10) | copy-start | bytes 2359300
  149.7 1.4 copy-start

commit v3 on v2

--- a/solution.py
+++ b/solution.py
@@ -167,9 +167,36 @@
     swap_cot = start(copy(cot.at[theirs], acts.at[1, 0, 1], x_send.at[1], x_recv.at[1], x_peer))
 
     pieces = [acts.at[0], acts.at[1], table]
-
-    def z_copy(p, k):
-        return copy(pieces[p].at[0], pieces[p].at[4 - k], z_send.at[p, k - 1], z_recv.at[p, 3 - k], z_peers[k - 1])
+    up_peer = ((z_pos + 1) % 4 * 4 + e % 4, d)
+    down_peer = ((z_pos + 3) % 4 * 4 + e % 4, d)
+    guarded = []
+
+    def line_copy(p, base, src, dst, send, peer):
+        return copy(
+            pieces[p].at[base + src],
+            pieces[p].at[base + dst],
+            z_send.at[p, base // 4, send],
+            z_recv.at[p, base // 4, dst - 1],
+            peer,
+        )
+
+    def start_when(condition, item):
+        pl.when(condition)(item.start)
+        guarded.append((condition, item))
+
+    def line_start(p, base):
+        start_when(z_pos < 3, line_copy(p, base, 0, 3, 0, up_peer))
+        start_when(z_pos > 0, line_copy(p, base, 0, 1, 1, down_peer))
+
+    def line_step(p, base, j):
+        line_copy(p, base, 0, j, 0, up_peer).wait_recv()
+        if j == 1:
+            start_when((z_pos > 0) & (z_pos < 3), line_copy(p, base, 1, 2, 2, down_peer))
+        elif j == 3:
+            start_when((z_pos > 0) & (z_pos < 3), line_copy(p, base, 3, 2, 3, up_peer))
+        else:
+            start_when(z_pos == 1, line_copy(p, base, 2, 3, 4, down_peer))
+            start_when(z_pos == 2, line_copy(p, base, 2, 1, 4, up_peer))
 
     def y_copy(p, j):
         return copy(pieces[p].at[j], pieces[p].at[4 + j], y_send.at[p, j], y_recv.at[p, j], y_peer)
@@ -177,36 +204,39 @@
     def c_copy(p, j):
         return copy(pieces[p].at[j], pieces[p].at[8 + j], c_send.at[p, j], c_recv.at[p, j], core_peer)
 
-    def spread_own(p):
-        for k in (2, 1, 3):
-            start(z_copy(p, k))
+    for p in (2, 0):
+        line_start(p, 0)
         start(y_copy(p, 0))
         start(c_copy(p, 0))
-
-    def forward(p):
-        for j in (1, 3, 2):
-            z_copy(p, 4 - j).wait_recv()
-            start(y_copy(p, j))
-            start(c_copy(p, j))
-        for j in (0, 1, 3, 2):
-            y_copy(p, j).wait_recv()
-            start(c_copy(p, 4 + j))
-
-    spread_own(2)
-    spread_own(0)
+    w_own[:, :width] = wg[...]
+    w_own[:, width:] = wu[...]
     swap_tok.wait_recv()
     swap_cot.wait_recv()
-    spread_own(1)
+    start(y_copy(1, 0))
+    line_start(1, 0)
+    start(c_copy(1, 0))
     w_copies = [
         start(copy(wg, w_far.at[:, pl.ds(0, width)], x_send.at[2], x_recv.at[2], x_peer)),
         start(copy(wu, w_far.at[:, pl.ds(width, width)], x_send.at[3], x_recv.at[3], x_peer)),
     ]
-    w_own[:, :width] = wg[...]
-    w_own[:, width:] = wu[...]
-    forward(2)
-    forward(0)
     down_copy = start(copy(wd, wd_far, x_send.at[4], x_recv.at[4], x_peer))
-    forward(1)
+    for j in (1, 3, 2):
+        for p in (2, 0):
+            line_step(p, 0, j)
+            start(y_copy(p, j))
+            start(c_copy(p, j))
+        if j == 3:
+            y_copy(1, 0).wait_recv()
+            line_start(1, 4)
+            start(c_copy(1, 4))
+    for j in (1, 3, 2):
+        for base in (0, 4):
+            line_step(1, base, j)
+            start(c_copy(1, base + j))
+    for j in (0, 1, 3, 2):
+        for p in (2, 0):
+            y_copy(p, j).wait_recv()
+            start(c_copy(p, 4 + j))
     for p in (2, 0, 1):
         for j in range(8):
             c_copy(p, j).wait_recv()
@@ -282,6 +312,12 @@
 
     rows_back(1, 2)
     start(rc_copy(1))
+    rows_back(0, 2)
+    start(rc_copy(0))
+    rows_back(1, 0)
+    rc_copy(1).wait_recv()
+    add_into(1, 4, from_core, 4)
+    start(ry_copy(1))
 
     @pl.loop(0, 4)
     def _(i):
@@ -293,17 +329,11 @@
     grad_copies.append(start(copy(gate_send, gate_far, x_send.at[6], x_recv.at[6], x_peer)))
     grad_copies.append(start(copy(up_send, up_far, x_send.at[7], x_recv.at[7], x_peer)))
 
-    rows_back(1, 0)
-    rc_copy(1).wait_recv()
-    add_into(1, 4, from_core, 4)
-    start(ry_copy(1))
-    rows_back(0, 2)
-    start(rc_copy(0))
     rows_back(0, 0)
-    add_into(1, 0, from_core, 0)
     rc_copy(0).wait_recv()
     add_into(0, 4, from_core, 4)
     start(ry_copy(0))
+    add_into(1, 0, from_core, 0)
     add_into(0, 0, from_core, 0)
 
     ry_copy(1).wait_recv()
@@ -344,6 +374,8 @@
     out_tok[theirs, :] = tok_far[...]
     for item in sends:
         item.wait_send()
+    for condition, item in guarded:
+        pl.when(condition)(item.wait_send)
 
 
 def dense_shards(tokens, grad_out, routes, gates, w_gate, w_up, w_down):
@@ -392,7 +424,7 @@
             pltpu.VMEM((feats, width), bf),
             pltpu.VMEM((width, feats), bf),
             dma((9,)), dma((9,)),
-            dma((3, 3)), dma((3, 3)),
+            dma((3, 2, 5)), dma((3, 2, 3)),
             dma((3, 4)), dma((3, 4)),
             dma((3, 8)), dma((3, 8)),
             dma((2,)), dma((2,)),

time: 152 us -> 140 us (0.921)
  the two profiles are of different devices: /device:TPU:9 before, /device:TPU:25 now
where the time goes in v3:
time: 140 us; the launch traced here: 139 us
  Pallas kernels  130 us (93%)
  local copies, waits for them, and re-layouts  7.6 us (5%)
    pallas_call x1, Pallas kernels, dense_shards(): pl.pallas_call(fused_kernel, out_shape=(jax.ShapeDtypeStruct((tok_count,...  130 us
    unnamed x14, local copies, waits for them, and re-layouts  7.6 us

profile of v3, /device:TPU:25, one launch (start us, length us, event | category | flops | bytes accessed | tf_op | source)
XLA Modules:
  0.0 139.3 jit_solution(3083246116642823780)
XLA Ops:
  0.6 0.0 copy-start.2
  0.6 0.7 copy-done.2
  1.3 0.0 copy-start.3
  1.3 0.1 copy.13
  1.4 0.6 copy-done.3
  2.0 0.1 copy.14
  2.1 1.0 select_reduce_fusion.tab
  3.1 130.0 %shard_map.102 = (bf16[128,1024]{1,0:T(8,128)(2,1)}, bf16[1024,384]{1,0:T(8,128)(2,1)}, bf16[1024,384]{1,0:T(8,128)(2,1)}, bf16[384,1024]{1,0:T(8,128)(2,1)}) custom-call(bf16[128,1024]{1,0:T(8,128)(2,1)} %tok.1, bf16[128,1024]{1,0:T(8,128)(2,1)} %cot.1, f32[128,128]{1,0:T(8,128)} %select_reduce_fusion.tab, bf16[1024,384]{1,0:T(8,128)(2,1)} %bitcast.9, ...), custom_call_target="tpu_custom_call" | custom-call | flops 12884901888 | bytes 8388608 | tf_op jit(solution)/shard_map/pallas_call | solution.py:392
  133.1 1.7 %copy.19 = bf16[128,1024]{1,0:T(8,128)(2,1)} copy(bf16[128,1024]{1,0:T(8,128)(2,1)} %get-tuple-element.16) | data formatting | bytes 524288
  134.8 0.0 copy-start.1
  134.8 2.2 %copy.20 = bf16[1,1024,384]{2,1,0:T(8,128)(2,1)} copy(bf16[1,1024,384]{2,1,0:T(8,128)(2,1)} %bitcast.8) | data formatting | bytes 1572864
  137.0 0.0 copy-done.1
  137.0 0.0 copy-start
  137.0 0.9 copy.21
  137.8 0.5 copy-done
  138.4 0.9 copy.22
Async XLA Ops:
  0.6 0.7 copy-start.2
  1.3 0.7 copy-start.3
  134.8 2.2 %copy-start.1 = (bf16[1024,384]{1,0:T(8,128)(2,1)S(1)}, bf16[1024,384]{1,0:T(8,128)(2,1)}, u32[]{:S(2)}) copy-start(bf16[1024,384]{1,0:T(8,128)(2,1)} %get-tuple-element.10) | copy-start | bytes 2359300
  137.0 1.4 %copy-start = (bf16[384,1024]{1,0:T(8,128)(2,1)S(1)}, bf16[384,1024]{1,0:T(8,128)(2,1)}, u32[]{:S(2)}) copy-start(bf16[384,1024]{1,0:T(8,128)(2,1)} %get-tuple-element.11) | copy-start | bytes 2359300

commit v4 on v3

--- a/solution.py
+++ b/solution.py
@@ -119,7 +119,7 @@
 
 
 def fused_kernel(
-    tok, cot, tab, wg, wu, wd,
+    tok, cot, routes, gates, wg, wu, wd,
     out_tok, out_gate, out_up, out_down,
     acts, table, w_own, w_far, wd_far, scaled, pre, hidden, d_both,
     row_grad, from_core, from_y, from_z, tok_send, tok_far,
@@ -153,7 +153,12 @@
     theirs = pl.ds(pl.multiple_of((1 - d) * half, half), half)
     acts[0, 0, 0] = tok[mine, :]
     acts[0, 0, 1] = cot[mine, :]
-    table[0] = tab[mine, :]
+    lanes = lax.broadcasted_iota(jnp.int32, (half, table.shape[-1]), 1)
+    chosen, weight = routes[mine, :], gates[mine, :]
+    own_table = jnp.zeros((half, table.shape[-1]), jnp.float32)
+    for k in range(routes.shape[1]):
+        own_table += jnp.where(lanes == chosen[:, k : k + 1], weight[:, k : k + 1], 0.0)
+    table[0] = own_table
     pl.semaphore_wait(barrier, 6)
 
     sends = []
@@ -166,15 +171,19 @@
     swap_tok = start(copy(tok.at[theirs], acts.at[1, 0, 0], x_send.at[0], x_recv.at[0], x_peer))
     swap_cot = start(copy(cot.at[theirs], acts.at[1, 0, 1], x_send.at[1], x_recv.at[1], x_peer))
 
-    pieces = [acts.at[0], acts.at[1], table]
+    def piece(p, j):
+        if p == 2:
+            return table.at[j]
+        return acts.at[0, j] if p == 0 else acts.at[1, j, p // 3]
+
     up_peer = ((z_pos + 1) % 4 * 4 + e % 4, d)
     down_peer = ((z_pos + 3) % 4 * 4 + e % 4, d)
     guarded = []
 
     def line_copy(p, base, src, dst, send, peer):
         return copy(
-            pieces[p].at[base + src],
-            pieces[p].at[base + dst],
+            piece(p, base + src),
+            piece(p, base + dst),
             z_send.at[p, base // 4, send],
             z_recv.at[p, base // 4, dst - 1],
             peer,
@@ -199,10 +208,10 @@
             start_when(z_pos == 2, line_copy(p, base, 2, 1, 4, up_peer))
 
     def y_copy(p, j):
-        return copy(pieces[p].at[j], pieces[p].at[4 + j], y_send.at[p, j], y_recv.at[p, j], y_peer)
+        return copy(piece(p, j), piece(p, 4 + j), y_send.at[p, j], y_recv.at[p, j], y_peer)
 
     def c_copy(p, j):
-        return copy(pieces[p].at[j], pieces[p].at[8 + j], c_send.at[p, j], c_recv.at[p, j], core_peer)
+        return copy(piece(p, j), piece(p, 8 + j), c_send.at[p, j], c_recv.at[p, j], core_peer)
 
     for p in (2, 0):
         line_start(p, 0)
@@ -211,60 +220,90 @@
     w_own[:, :width] = wg[...]
     w_own[:, width:] = wu[...]
     swap_tok.wait_recv()
+    line_start(1, 0)
+    start(y_copy(1, 0))
+    start(c_copy(1, 0))
     swap_cot.wait_recv()
-    start(y_copy(1, 0))
-    line_start(1, 0)
-    start(c_copy(1, 0))
+    start(y_copy(3, 0))
+    line_start(3, 0)
+    start(c_copy(3, 0))
     w_copies = [
         start(copy(wg, w_far.at[:, pl.ds(0, width)], x_send.at[2], x_recv.at[2], x_peer)),
         start(copy(wu, w_far.at[:, pl.ds(width, width)], x_send.at[3], x_recv.at[3], x_peer)),
     ]
     down_copy = start(copy(wd, wd_far, x_send.at[4], x_recv.at[4], x_peer))
+
+    tile = 4 * half
+    blocks = 4
+
+    def rows_of(i):
+        return pl.ds(pl.multiple_of(i * tile, tile), tile)
+
+    def scale_rows(h, i):
+        rows, group = rows_of(i), pl.ds(i * 4, 4)
+        lanes = lax.broadcasted_iota(jnp.int32, (tile, table.shape[-1]), 1)
+        column = jnp.sum(
+            jnp.where(lanes == e, table[group].reshape(tile, -1), 0.0), axis=1, keepdims=True
+        )
+        value = acts[h, group, 1].reshape(tile, feats).astype(jnp.float32)
+        scaled[h, rows, :] = (value * column).astype(jnp.bfloat16)
+
+    def near_rows(first, count):
+        @pl.loop(first, first + count)
+        def _(i):
+            left = acts[0, pl.ds(i * 4, 4), 0].reshape(tile, feats)
+            pre[rows_of(i), :] = jnp.dot(left, w_own[...], preferred_element_type=jnp.float32)
+            scale_rows(0, i)
+
     for j in (1, 3, 2):
         for p in (2, 0):
             line_step(p, 0, j)
             start(y_copy(p, j))
             start(c_copy(p, j))
         if j == 3:
-            y_copy(1, 0).wait_recv()
-            line_start(1, 4)
-            start(c_copy(1, 4))
+            y_copy(3, 0).wait_recv()
+            line_start(3, 4)
+            start(c_copy(3, 4))
     for j in (1, 3, 2):
-        for base in (0, 4):
-            line_step(1, base, j)
-            start(c_copy(1, base + j))
+        line_step(1, 0, j)
+        start(y_copy(1, j))
+        start(c_copy(1, j))
     for j in (0, 1, 3, 2):
         for p in (2, 0):
             y_copy(p, j).wait_recv()
             start(c_copy(p, 4 + j))
-    for p in (2, 0, 1):
+    near_rows(0, 2)
+    for p in (2, 0):
         for j in range(8):
             c_copy(p, j).wait_recv()
+    near_rows(2, 2)
+    for j in (1, 3, 2):
+        for base in (0, 4):
+            line_step(3, base, j)
+            start(c_copy(3, base + j))
+    for j in (0, 1, 3, 2):
+        y_copy(1, j).wait_recv()
+        start(c_copy(1, 4 + j))
+    for j in range(8):
+        c_copy(1, j).wait_recv()
     for item in w_copies:
         item.wait_recv()
 
-    tile = 4 * half
-    blocks = 4
-
-    def rows_of(i):
-        return pl.ds(pl.multiple_of(i * tile, tile), tile)
-
     @pl.loop(0, blocks)
     def _(i):
-        rows, group = rows_of(i), pl.ds(i * 4, 4)
-        lanes = lax.broadcasted_iota(jnp.int32, (tile, table.shape[-1]), 1)
-        column = jnp.sum(
-            jnp.where(lanes == e, table[group].reshape(tile, -1), 0.0), axis=1, keepdims=True
-        )
-        for h in range(2):
-            far = acts[h, group, 1].reshape(tile, feats).astype(jnp.float32)
-            scaled[h, rows, :] = (far * column).astype(jnp.bfloat16)
-        near = jnp.dot(acts[0, group, 0].reshape(tile, feats), w_own[...], preferred_element_type=jnp.float32)
-        far = jnp.dot(acts[1, group, 0].reshape(tile, feats), w_far[...], preferred_element_type=jnp.float32)
-        total = near + far
+        rows = rows_of(i)
+        left = acts[1, pl.ds(i * 4, 4), 0].reshape(tile, feats)
+        total = pre[rows, :] + jnp.dot(left, w_far[...], preferred_element_type=jnp.float32)
         pre[rows, :] = total
         gate, up = total[:, :width], total[:, width:]
         hidden[rows, :] = (gate * jax.nn.sigmoid(gate) * up).astype(jnp.bfloat16)
+
+    for j in range(8):
+        c_copy(3, j).wait_recv()
+
+    @pl.loop(0, blocks)
+    def _(i):
+        scale_rows(1, i)
 
     strip = feats // 4
 
@@ -287,6 +326,8 @@
         d_both[rows, :width] = (back * up * sig * (1.0 + gate * (1.0 - sig))).astype(jnp.bfloat16)
         d_both[rows, width:] = (back * (gate * sig)).astype(jnp.bfloat16)
 
+    chunk = feats // 2
+
     def rc_copy(h):
         return copy(row_grad.at[h, pl.ds(8, 8)], from_core.at[h], rc_send.at[h], rc_recv.at[h], core_peer)
 
@@ -296,28 +337,53 @@
     def rz_copy(h, k):
         return copy(row_grad.at[h, k], from_z.at[h, 3 - k], rz_send.at[h, k - 1], rz_recv.at[h, 3 - k], z_peers[k - 1])
 
-    def rows_back(h, first):
-        weights = w_own if h == 0 else w_far
+    def rows_back(q, first):
+        weights = w_own if q < 2 else w_far
+        part = pl.ds(q % 2 * chunk, chunk)
 
         @pl.loop(first, first + 2)
         def _(i):
-            value = contract_cols(d_both[rows_of(i), :], weights[...])
-            row_grad[h, pl.ds(i * 4, 4)] = value.astype(jnp.bfloat16).reshape(4, half, feats)
-
-    def add_into(h, first, extra, offset):
+            value = contract_cols(d_both[rows_of(i), :], weights[part, :])
+            row_grad[q, pl.ds(i * 4, 4)] = value.astype(jnp.bfloat16).reshape(4, half, chunk)
+
+    def to_y(q):
+        rows_back(q, 0)
+        rc_copy(q).wait_recv()
+
+        @pl.loop(4, 8)
+        def _(j):
+            near = row_grad[q, j].astype(jnp.float32)
+            row_grad[q, j] = (near + from_core[q, j].astype(jnp.float32)).astype(jnp.bfloat16)
+
+        start(ry_copy(q))
+
+    def to_z(q):
+        ry_copy(q).wait_recv()
+
         @pl.loop(0, 4)
         def _(j):
-            near = row_grad[h, first + j].astype(jnp.float32)
-            row_grad[h, first + j] = (near + extra[h, offset + j].astype(jnp.float32)).astype(jnp.bfloat16)
-
-    rows_back(1, 2)
-    start(rc_copy(1))
-    rows_back(0, 2)
-    start(rc_copy(0))
-    rows_back(1, 0)
-    rc_copy(1).wait_recv()
-    add_into(1, 4, from_core, 4)
-    start(ry_copy(1))
+            near = row_grad[q, j].astype(jnp.float32) + from_core[q, j].astype(jnp.float32)
+            row_grad[q, j] = (near + from_y[q, j].astype(jnp.float32)).astype(jnp.bfloat16)
+
+        for k in (2, 1, 3):
+            start(rz_copy(q, k))
+
+    def finish(q):
+        total = row_grad[q, 0].astype(jnp.float32)
+        for k in range(3):
+            rz_copy(q, 3 - k).wait_recv()
+        for k in range(3):
+            total = total + from_z[q, k].astype(jnp.float32)
+        return total.astype(jnp.bfloat16)
+
+    for q in (2, 3):
+        rows_back(q, 2)
+        start(rc_copy(q))
+    to_y(2)
+    for q in (0, 1):
+        rows_back(q, 2)
+        start(rc_copy(q))
+    to_y(3)
 
     @pl.loop(0, 4)
     def _(i):
@@ -329,17 +395,10 @@
     grad_copies.append(start(copy(gate_send, gate_far, x_send.at[6], x_recv.at[6], x_peer)))
     grad_copies.append(start(copy(up_send, up_far, x_send.at[7], x_recv.at[7], x_peer)))
 
-    rows_back(0, 0)
-    rc_copy(0).wait_recv()
-    add_into(0, 4, from_core, 4)
-    start(ry_copy(0))
-    add_into(1, 0, from_core, 0)
-    add_into(0, 0, from_core, 0)
-
-    ry_copy(1).wait_recv()
-    add_into(1, 0, from_y, 0)
-    for k in (2, 1, 3):
-        start(rz_copy(1, k))
+    to_y(0)
+    to_z(2)
+    to_y(1)
+    to_z(3)
 
     @pl.loop(0, 4)
     def _(i):
@@ -347,25 +406,15 @@
         gate_own[cols_of(i), :] = contract_first(left, d_both[...])
         down_own[:, cols_of(i)] = contract_first(hidden[...], scaled[0, :, cols_of(i)])
 
-    ry_copy(0).wait_recv()
-    add_into(0, 0, from_y, 0)
-    for k in (2, 1, 3):
-        start(rz_copy(0, k))
-
-    def finish(h):
-        total = row_grad[h, 0].astype(jnp.float32)
-        for k in range(3):
-            rz_copy(h, 3 - k).wait_recv()
-        for k in range(3):
-            total = total + from_z[h, k].astype(jnp.float32)
-        return total.astype(jnp.bfloat16)
-
-    tok_send[...] = finish(1)
+    to_z(0)
+    tok_send[:, :chunk] = finish(2)
+    to_z(1)
+    tok_send[:, chunk:] = finish(3)
     tok_copy = start(copy(tok_send, tok_far, x_send.at[8], x_recv.at[8], x_peer))
-    out_tok[mine, :] = finish(0)
-
     grad_copies[0].wait_recv()
     out_down[...] = (down_own[...] + down_far[...].astype(jnp.float32)).astype(jnp.bfloat16)
+    out_tok[mine, :chunk] = finish(0)
+    out_tok[mine, chunk:] = finish(1)
     grad_copies[1].wait_recv()
     out_gate[...] = (gate_own[:, :width] + gate_far[...].astype(jnp.float32)).astype(jnp.bfloat16)
     grad_copies[2].wait_recv()
@@ -378,18 +427,27 @@
         pl.when(condition)(item.wait_send)
 
 
+def copy_kernel(*refs):
+    count = len(refs) // 2
+    items = [
+        pltpu.make_async_copy(refs[i], refs[count + i], refs[-1].at[i]) for i in range(count)
+    ]
+    for item in items:
+        item.start()
+    for item in items:
+        item.wait()
+
+
 def dense_shards(tokens, grad_out, routes, gates, w_gate, w_up, w_down):
     experts = lax.axis_size("expert")
     tok_count, feats = tokens.shape
     width = w_gate.shape[2]
     half = tok_count // 2
-    named = routes[:, :, None] == jnp.arange(128, dtype=jnp.int32)
-    table = jnp.sum(jnp.where(named, gates[:, :, None], 0.0), axis=1)
     bf, f32 = jnp.bfloat16, jnp.float32
     rows = experts * half
     vmem = pl.BlockSpec(memory_space=pltpu.VMEM)
     dma = pltpu.SemaphoreType.DMA
-    d_tokens, grad_gate, grad_up, grad_down = pl.pallas_call(
+    results = pl.pallas_call(
         fused_kernel,
         out_shape=(
             jax.ShapeDtypeStruct((tok_count, feats), bf),
@@ -397,7 +455,7 @@
             jax.ShapeDtypeStruct((feats, width), bf),
             jax.ShapeDtypeStruct((width, feats), bf),
         ),
-        in_specs=[vmem] * 6,
+        in_specs=[vmem] * 7,
         out_specs=(vmem,) * 4,
         scratch_shapes=[
             pltpu.VMEM((2, experts, 2, half, feats), bf),
@@ -409,10 +467,10 @@
             pltpu.VMEM((rows, 2 * width), f32),
             pltpu.VMEM((rows, width), bf),
             pltpu.VMEM((rows, 2 * width), bf),
-            pltpu.VMEM((2, experts, half, feats), bf),
-            pltpu.VMEM((2, 8, half, feats), bf),
-            pltpu.VMEM((2, 4, half, feats), bf),
-            pltpu.VMEM((2, 3, half, feats), bf),
+            pltpu.VMEM((4, experts, half, feats // 2), bf),
+            pltpu.VMEM((4, 8, half, feats // 2), bf),
+            pltpu.VMEM((4, 4, half, feats // 2), bf),
+            pltpu.VMEM((4, 3, half, feats // 2), bf),
             pltpu.VMEM((half, feats), bf),
             pltpu.VMEM((half, feats), bf),
             pltpu.VMEM((feats, 2 * width), f32),
@@ -424,12 +482,12 @@
             pltpu.VMEM((feats, width), bf),
             pltpu.VMEM((width, feats), bf),
             dma((9,)), dma((9,)),
-            dma((3, 2, 5)), dma((3, 2, 3)),
-            dma((3, 4)), dma((3, 4)),
-            dma((3, 8)), dma((3, 8)),
-            dma((2,)), dma((2,)),
-            dma((2,)), dma((2,)),
-            dma((2, 3)), dma((2, 3)),
+            dma((4, 2, 5)), dma((4, 2, 3)),
+            dma((4, 4)), dma((4, 4)),
+            dma((4, 8)), dma((4, 8)),
+            dma((4,)), dma((4,)),
+            dma((4,)), dma((4,)),
+            dma((4, 3)), dma((4, 3)),
         ],
         compiler_params=pltpu.CompilerParams(
             collective_id=0, has_side_effects=True, vmem_limit_bytes=60 * 1024 * 1024
@@ -437,7 +495,15 @@
         cost_estimate=pl.CostEstimate(
             flops=16 * rows * 2 * feats * width, bytes_accessed=8 * 1024 * 1024, transcendentals=rows * width
         ),
-    )(tokens, grad_out, table, w_gate[0], w_up[0], w_down[0])
+    )(tokens, grad_out, routes, gates, w_gate[0], w_up[0], w_down[0])
+    anywhere = pl.BlockSpec(memory_space=pl.ANY)
+    d_tokens, grad_gate, grad_up, grad_down = pl.pallas_call(
+        copy_kernel,
+        out_shape=tuple(jax.ShapeDtypeStruct(r.shape, r.dtype) for r in results),
+        in_specs=[anywhere] * 4,
+        out_specs=(anywhere,) * 4,
+        scratch_shapes=[dma((4,))],
+    )(*results)
     return (d_tokens, grad_gate[None], grad_up[None], grad_down[None])
 
 

time: 140 us -> 208 us (1.49)
  Pallas kernels: 130 us -> 205 us
  local copies, waits for them, and re-layouts: 7.6 us -> 2.14 us
    pallas_call x0 -> x1, Pallas kernels: none -> 80.5 us  [dense_shards(): pl.pallas_call(copy_kernel, out_shape=tuple((jax.ShapeDtypeStruct(r.shape...]
    pallas_call x1, Pallas kernels: 130 us -> 124 us  [dense_shards(): pl.pallas_call(fused_kernel, out_shape=(jax.ShapeDtypeStruct((tok_count,...]
    unnamed x14 -> x6, local copies, waits for them, and re-layouts: 7.6 us -> 2.14 us
where the time goes in v4:
time: 208 us
  Pallas kernels  205 us (99%)
  local copies, waits for them, and re-layouts  2.14 us (1%)
    pallas_call x1, Pallas kernels, dense_shards(): pl.pallas_call(fused_kernel, out_shape=(jax.ShapeDtypeStruct((tok_count,...  124 us
    pallas_call x1, Pallas kernels, dense_shards(): pl.pallas_call(copy_kernel, out_shape=tuple((jax.ShapeDtypeStruct(r.shape...  80.5 us

profile of v4, /device:TPU:25, one launch (start us, length us, event | category | flops | bytes accessed | tf_op | source)
XLA Modules:
  0.0 207.6 jit_solution(7319732871561893612)
XLA Ops:
  0.6 0.0 copy-start
  0.6 0.7 copy-done
  1.3 0.0 copy-start.1
  1.3 0.7 copy.11.routes
  2.0 0.0 copy-done.1
  2.1 0.7 copy.12.gates
  2.8 124.3 %shard_map.102 = (bf16[128,1024]{1,0:T(8,128)(2,1)}, bf16[1024,384]{1,0:T(8,128)(2,1)}, bf16[1024,384]{1,0:T(8,128)(2,1)}, bf16[384,1024]{1,0:T(8,128)(2,1)}) custom-call(bf16[128,1024]{1,0:T(8,128)(2,1)} %tok.1, bf16[128,1024]{1,0:T(8,128)(2,1)} %cot.1, s32[128,8]{1,0:T(8,128)} %copy.11.routes, f32[128,8]{1,0:T(8,128)} %copy.12.gates, ...), custom_call_target="tpu_custom_call" | custom-call | flops 12884901888 | bytes 8388608 | tf_op jit(solution)/shard_map/pallas_call | solution.py:450
  127.1 80.5 %shard_map.103 = (bf16[128,1024]{1,0:T(8,128)(2,1)}, bf16[1024,384]{1,0:T(8,128)(2,1)}, bf16[1024,384]{1,0:T(8,128)(2,1)}, bf16[384,1024]{1,0:T(8,128)(2,1)}) custom-call(bf16[128,1024]{1,0:T(8,128)(2,1)} %get-tuple-element.12.refs_0_, bf16[1024,384]{1,0:T(8,128)(2,1)} %get-tuple-element.13.refs_1_, bf16[1024,384]{1,0:T(8,128)(2,1)} %get-tuple-element.14.refs_2_, ...), custom_call_target="tpu_custom_call" | custom-call | tf_op jit(solution)/shard_map/pallas_call | solution.py:500
Async XLA Ops:
  0.6 0.7 copy-start
  1.3 0.7 copy-start.1

commit v5 on v4

--- a/solution.py
+++ b/solution.py
@@ -123,7 +123,7 @@
     out_tok, out_gate, out_up, out_down,
     acts, table, w_own, w_far, wd_far, scaled, pre, hidden, d_both,
     row_grad, from_core, from_y, from_z, tok_send, tok_far,
-    gate_own, down_own, gate_send, up_send, down_send, gate_far, up_far, down_far,
+    both_own, down_own, both_send, down_send, both_far, down_far, named_rows, gate_rows,
     x_send, x_recv, z_send, z_recv, y_send, y_recv, c_send, c_recv,
     rc_send, rc_recv, ry_send, ry_recv, rz_send, rz_recv,
 ):
@@ -154,9 +154,11 @@
     acts[0, 0, 0] = tok[mine, :]
     acts[0, 0, 1] = cot[mine, :]
     lanes = lax.broadcasted_iota(jnp.int32, (half, table.shape[-1]), 1)
-    chosen, weight = routes[mine, :], gates[mine, :]
+    named_rows[...] = jnp.transpose(routes[...])
+    gate_rows[...] = jnp.transpose(gates[...])
+    chosen, weight = named_rows[mine, :], gate_rows[mine, :]
     own_table = jnp.zeros((half, table.shape[-1]), jnp.float32)
-    for k in range(routes.shape[1]):
+    for k in range(routes.shape[0]):
         own_table += jnp.where(lanes == chosen[:, k : k + 1], weight[:, k : k + 1], 0.0)
     table[0] = own_table
     pl.semaphore_wait(barrier, 6)
@@ -219,6 +221,7 @@
         start(c_copy(p, 0))
     w_own[:, :width] = wg[...]
     w_own[:, width:] = wu[...]
+    w_copies = [start(copy(wg, w_far.at[:, pl.ds(0, width)], x_send.at[2], x_recv.at[2], x_peer))]
     swap_tok.wait_recv()
     line_start(1, 0)
     start(y_copy(1, 0))
@@ -227,10 +230,9 @@
     start(y_copy(3, 0))
     line_start(3, 0)
     start(c_copy(3, 0))
-    w_copies = [
-        start(copy(wg, w_far.at[:, pl.ds(0, width)], x_send.at[2], x_recv.at[2], x_peer)),
-        start(copy(wu, w_far.at[:, pl.ds(width, width)], x_send.at[3], x_recv.at[3], x_peer)),
-    ]
+    w_copies.append(
+        start(copy(wu, w_far.at[:, pl.ds(width, width)], x_send.at[3], x_recv.at[3], x_peer))
+    )
     down_copy = start(copy(wd, wd_far, x_send.at[4], x_recv.at[4], x_peer))
 
     tile = 4 * half
@@ -376,25 +378,27 @@
             total = total + from_z[q, k].astype(jnp.float32)
         return total.astype(jnp.bfloat16)
 
+    def far_grads(part):
+        @pl.loop(2 * part, 2 * part + 2)
+        def _(i):
+            left = acts[1, :, 0, :, cols_of(i)].reshape(16 * half, strip)
+            both_send[cols_of(i), :] = contract_first(left, d_both[...]).astype(jnp.bfloat16)
+
+        rows = pl.ds(part * chunk, chunk)
+        grad_copies.append(
+            start(copy(both_send.at[rows], both_far.at[rows], x_send.at[6 + part], x_recv.at[6 + part], x_peer))
+        )
+
     for q in (2, 3):
         rows_back(q, 2)
         start(rc_copy(q))
     to_y(2)
+    far_grads(0)
     for q in (0, 1):
         rows_back(q, 2)
         start(rc_copy(q))
     to_y(3)
-
-    @pl.loop(0, 4)
-    def _(i):
-        left = acts[1, :, 0, :, cols_of(i)].reshape(16 * half, strip)
-        value = contract_first(left, d_both[...]).astype(jnp.bfloat16)
-        gate_send[cols_of(i), :] = value[:, :width]
-        up_send[cols_of(i), :] = value[:, width:]
-
-    grad_copies.append(start(copy(gate_send, gate_far, x_send.at[6], x_recv.at[6], x_peer)))
-    grad_copies.append(start(copy(up_send, up_far, x_send.at[7], x_recv.at[7], x_peer)))
-
+    far_grads(1)
     to_y(0)
     to_z(2)
     to_y(1)
@@ -403,7 +407,7 @@
     @pl.loop(0, 4)
     def _(i):
         left = acts[0, :, 0, :, cols_of(i)].reshape(16 * half, strip)
-        gate_own[cols_of(i), :] = contract_first(left, d_both[...])
+        both_own[cols_of(i), :] = contract_first(left, d_both[...])
         down_own[:, cols_of(i)] = contract_first(hidden[...], scaled[0, :, cols_of(i)])
 
     to_z(0)
@@ -415,10 +419,12 @@
     out_down[...] = (down_own[...] + down_far[...].astype(jnp.float32)).astype(jnp.bfloat16)
     out_tok[mine, :chunk] = finish(0)
     out_tok[mine, chunk:] = finish(1)
-    grad_copies[1].wait_recv()
-    out_gate[...] = (gate_own[:, :width] + gate_far[...].astype(jnp.float32)).astype(jnp.bfloat16)
-    grad_copies[2].wait_recv()
-    out_up[...] = (gate_own[:, width:] + up_far[...].astype(jnp.float32)).astype(jnp.bfloat16)
+    for part in range(2):
+        rows = pl.ds(part * chunk, chunk)
+        grad_copies[1 + part].wait_recv()
+        total = (both_own[rows, :] + both_far[rows, :].astype(jnp.float32)).astype(jnp.bfloat16)
+        out_gate[rows, :] = total[:, :width]
+        out_up[rows, :] = total[:, width:]
     tok_copy.wait_recv()
     out_tok[theirs, :] = tok_far[...]
     for item in sends:
@@ -429,13 +435,8 @@
 
 def copy_kernel(*refs):
     count = len(refs) // 2
-    items = [
-        pltpu.make_async_copy(refs[i], refs[count + i], refs[-1].at[i]) for i in range(count)
-    ]
-    for item in items:
-        item.start()
-    for item in items:
-        item.wait()
+    for i in range(count):
+        refs[count + i][...] = refs[i][...]
 
 
 def dense_shards(tokens, grad_out, routes, gates, w_gate, w_up, w_down):
@@ -475,12 +476,12 @@
             pltpu.VMEM((half, feats), bf),
             pltpu.VMEM((feats, 2 * width), f32),
             pltpu.VMEM((width, feats), f32),
-            pltpu.VMEM((feats, width), bf),
-            pltpu.VMEM((feats, width), bf),
+            pltpu.VMEM((feats, 2 * width), bf),
             pltpu.VMEM((width, feats), bf),
-            pltpu.VMEM((feats, width), bf),
-            pltpu.VMEM((feats, width), bf),
+            pltpu.VMEM((feats, 2 * width), bf),
             pltpu.VMEM((width, feats), bf),
+            pltpu.VMEM(routes.shape, jnp.int32),
+            pltpu.VMEM(gates.shape, f32),
             dma((9,)), dma((9,)),
             dma((4, 2, 5)), dma((4, 2, 3)),
             dma((4, 4)), dma((4, 4)),
@@ -495,14 +496,16 @@
         cost_estimate=pl.CostEstimate(
             flops=16 * rows * 2 * feats * width, bytes_accessed=8 * 1024 * 1024, transcendentals=rows * width
         ),
-    )(tokens, grad_out, routes, gates, w_gate[0], w_up[0], w_down[0])
-    anywhere = pl.BlockSpec(memory_space=pl.ANY)
+    )(tokens, grad_out, routes.T, gates.T, w_gate[0], w_up[0], w_down[0])
+    steps = 4
+    specs = [pl.BlockSpec((r.shape[0] // steps, r.shape[1]), lambda i: (i, 0)) for r in results]
     d_tokens, grad_gate, grad_up, grad_down = pl.pallas_call(
         copy_kernel,
+        grid=(steps,),
         out_shape=tuple(jax.ShapeDtypeStruct(r.shape, r.dtype) for r in results),
-        in_specs=[anywhere] * 4,
-        out_specs=(anywhere,) * 4,
-        scratch_shapes=[dma((4,))],
+        in_specs=specs,
+        out_specs=tuple(specs),
+        compiler_params=pltpu.CompilerParams(vmem_limit_bytes=60 * 1024 * 1024),
     )(*results)
     return (d_tokens, grad_gate[None], grad_up[None], grad_down[None])
 

time: 208 us -> 129 us (0.62)
  Pallas kernels: 205 us -> 128 us
  local copies, waits for them, and re-layouts: 2.14 us -> 0 us
    pallas_call x1, Pallas kernels: 80.5 us -> 4.04 us  [dense_shards(): pl.pallas_call(copy_kernel, grid=(steps,), out_shape=tuple((jax.ShapeDtyp...]
    unnamed x6 -> x0, local copies, waits for them, and re-layouts: 2.14 us -> none
where the time goes in v5:
time: 129 us
  Pallas kernels  128 us (99%)
    pallas_call x1, Pallas kernels, dense_shards(): pl.pallas_call(fused_kernel, out_shape=(jax.ShapeDtypeStruct((tok_count,...  124 us
    pallas_call x1, Pallas kernels, dense_shards(): pl.pallas_call(copy_kernel, grid=(steps,), out_shape=tuple((jax.ShapeDtyp...  4.04 us

profile of v5, /device:TPU:25, one launch (start us, length us, event | category | flops | bytes accessed | tf_op | source)
XLA Modules:
  0.0 128.9 jit_solution(11657967144734911751)
XLA Ops:
  0.6 124.3 %shard_map.102 = (bf16[128,1024]{1,0:T(8,128)(2,1)}, bf16[1024,384]{1,0:T(8,128)(2,1)}, bf16[1024,384]{1,0:T(8,128)(2,1)}, bf16[384,1024]{1,0:T(8,128)(2,1)}) custom-call(bf16[128,1024]{1,0:T(8,128)(2,1)} %tok.1, bf16[128,1024]{1,0:T(8,128)(2,1)} %cot.1, s32[8,128]{1,0:T(8,128)} %bitcast.14, f32[8,128]{1,0:T(8,128)} %bitcast.15, bf16[1024,384]{1,0:T(8,128)(2,1)} %bitcast.8, ...), custom_call_target="tpu_custom_call" | custom-call | flops 12884901888 | bytes 8388608 | tf_op jit(solution)/shard_map/pallas_call | solution.py:451
  124.9 4.0 %shard_map.103 = (bf16[128,1024]{1,0:T(8,128)(2,1)}, bf16[1024,384]{1,0:T(8,128)(2,1)}, bf16[1024,384]{1,0:T(8,128)(2,1)}, bf16[384,1024]{1,0:T(8,128)(2,1)}) custom-call(bf16[128,1024]{1,0:T(8,128)(2,1)} %get-tuple-element.12.refs_0_, bf16[1024,384]{1,0:T(8,128)(2,1)} %get-tuple-element.13.refs_1_, bf16[1024,384]{1,0:T(8,128)(2,1)} %get-tuple-element.14.refs_2_, ...), custom_call_target="tpu_custom_call" | custom-call | tf_op jit(solution)/shard_map/pallas_call | solution.py:502

commit v6 on v5

--- a/solution.py
+++ b/solution.py
@@ -124,6 +124,7 @@
     acts, table, w_own, w_far, wd_far, scaled, pre, hidden, d_both,
     row_grad, from_core, from_y, from_z, tok_send, tok_far,
     both_own, down_own, both_send, down_send, both_far, down_far, named_rows, gate_rows,
+    back_near, wd_own, local_sem,
     x_send, x_recv, z_send, z_recv, y_send, y_recv, c_send, c_recv,
     rc_send, rc_recv, ry_send, ry_recv, rz_send, rz_recv,
 ):
@@ -151,8 +152,20 @@
 
     mine = pl.ds(pl.multiple_of(d * half, half), half)
     theirs = pl.ds(pl.multiple_of((1 - d) * half, half), half)
-    acts[0, 0, 0] = tok[mine, :]
-    acts[0, 0, 1] = cot[mine, :]
+    own_copies = [
+        pltpu.make_async_copy(src, dst, local_sem.at[i])
+        for i, (src, dst) in enumerate(
+            [
+                (tok.at[mine], acts.at[0, 0, 0]),
+                (cot.at[mine], acts.at[0, 0, 1]),
+                (wg, w_own.at[:, pl.ds(0, width)]),
+                (wu, w_own.at[:, pl.ds(width, width)]),
+                (wd, wd_own),
+            ]
+        )
+    ]
+    for item in own_copies:
+        item.start()
     lanes = lax.broadcasted_iota(jnp.int32, (half, table.shape[-1]), 1)
     named_rows[...] = jnp.transpose(routes[...])
     gate_rows[...] = jnp.transpose(gates[...])
@@ -215,12 +228,12 @@
     def c_copy(p, j):
         return copy(piece(p, j), piece(p, 8 + j), c_send.at[p, j], c_recv.at[p, j], core_peer)
 
+    own_copies[0].wait()
+    own_copies[1].wait()
     for p in (2, 0):
         line_start(p, 0)
         start(y_copy(p, 0))
         start(c_copy(p, 0))
-    w_own[:, :width] = wg[...]
-    w_own[:, width:] = wu[...]
     w_copies = [start(copy(wg, w_far.at[:, pl.ds(0, width)], x_send.at[2], x_recv.at[2], x_peer))]
     swap_tok.wait_recv()
     line_start(1, 0)
@@ -256,6 +269,7 @@
             left = acts[0, pl.ds(i * 4, 4), 0].reshape(tile, feats)
             pre[rows_of(i), :] = jnp.dot(left, w_own[...], preferred_element_type=jnp.float32)
             scale_rows(0, i)
+            back_near[rows_of(i), :] = contract_cols(scaled[0, rows_of(i), :], wd_own[...])
 
     for j in (1, 3, 2):
         for p in (2, 0):
@@ -274,6 +288,8 @@
         for p in (2, 0):
             y_copy(p, j).wait_recv()
             start(c_copy(p, 4 + j))
+    for item in own_copies[2:]:
+        item.wait()
     near_rows(0, 2)
     for p in (2, 0):
         for j in range(8):
@@ -296,9 +312,11 @@
         rows = rows_of(i)
         left = acts[1, pl.ds(i * 4, 4), 0].reshape(tile, feats)
         total = pre[rows, :] + jnp.dot(left, w_far[...], preferred_element_type=jnp.float32)
-        pre[rows, :] = total
         gate, up = total[:, :width], total[:, width:]
-        hidden[rows, :] = (gate * jax.nn.sigmoid(gate) * up).astype(jnp.bfloat16)
+        sig = jax.nn.sigmoid(gate)
+        hidden[rows, :] = (gate * sig * up).astype(jnp.bfloat16)
+        pre[rows, :width] = up * sig * (1.0 + gate * (1.0 - sig))
+        pre[rows, width:] = gate * sig
 
     for j in range(8):
         c_copy(3, j).wait_recv()
@@ -322,11 +340,9 @@
     @pl.loop(0, blocks)
     def _(i):
         rows = rows_of(i)
-        back = contract_cols(scaled[0, rows, :], wd[...]) + contract_cols(scaled[1, rows, :], wd_far[...])
-        gate, up = pre[rows, :width], pre[rows, width:]
-        sig = jax.nn.sigmoid(gate)
-        d_both[rows, :width] = (back * up * sig * (1.0 + gate * (1.0 - sig))).astype(jnp.bfloat16)
-        d_both[rows, width:] = (back * (gate * sig)).astype(jnp.bfloat16)
+        back = back_near[rows, :] + contract_cols(scaled[1, rows, :], wd_far[...])
+        d_both[rows, :width] = (back * pre[rows, :width]).astype(jnp.bfloat16)
+        d_both[rows, width:] = (back * pre[rows, width:]).astype(jnp.bfloat16)
 
     chunk = feats // 2
 
@@ -434,9 +450,17 @@
 
 
 def copy_kernel(*refs):
-    count = len(refs) // 2
-    for i in range(count):
-        refs[count + i][...] = refs[i][...]
+    ins, outs, held = refs[0:4], refs[4:8], refs[8:12]
+    arrive, leave = refs[12:]
+    reads = [pltpu.make_async_copy(ins[i], held[i], arrive.at[i]) for i in range(4)]
+    writes = [pltpu.make_async_copy(held[i], outs[i], leave.at[i]) for i in range(4)]
+    for item in reads:
+        item.start()
+    for i in range(4):
+        reads[i].wait()
+        writes[i].start()
+    for item in writes:
+        item.wait()
 
 
 def dense_shards(tokens, grad_out, routes, gates, w_gate, w_up, w_down):
@@ -447,6 +471,7 @@
     bf, f32 = jnp.bfloat16, jnp.float32
     rows = experts * half
     vmem = pl.BlockSpec(memory_space=pltpu.VMEM)
+    anywhere = pl.BlockSpec(memory_space=pl.ANY)
     dma = pltpu.SemaphoreType.DMA
     results = pl.pallas_call(
         fused_kernel,
@@ -456,7 +481,7 @@
             jax.ShapeDtypeStruct((feats, width), bf),
             jax.ShapeDtypeStruct((width, feats), bf),
         ),
-        in_specs=[vmem] * 7,
+        in_specs=[anywhere] * 2 + [vmem] * 2 + [anywhere] * 3,
         out_specs=(vmem,) * 4,
         scratch_shapes=[
             pltpu.VMEM((2, experts, 2, half, feats), bf),
@@ -482,6 +507,9 @@
             pltpu.VMEM((width, feats), bf),
             pltpu.VMEM(routes.shape, jnp.int32),
             pltpu.VMEM(gates.shape, f32),
+            pltpu.VMEM((rows, width), f32),
+            pltpu.VMEM((width, feats), bf),
+            dma((5,)),
             dma((9,)), dma((9,)),
             dma((4, 2, 5)), dma((4, 2, 3)),
             dma((4, 4)), dma((4, 4)),
@@ -497,14 +525,12 @@
             flops=16 * rows * 2 * feats * width, bytes_accessed=8 * 1024 * 1024, transcendentals=rows * width
         ),
     )(tokens, grad_out, routes.T, gates.T, w_gate[0], w_up[0], w_down[0])
-    steps = 4
-    specs = [pl.BlockSpec((r.shape[0] // steps, r.shape[1]), lambda i: (i, 0)) for r in results]
     d_tokens, grad_gate, grad_up, grad_down = pl.pallas_call(
         copy_kernel,
-        grid=(steps,),
         out_shape=tuple(jax.ShapeDtypeStruct(r.shape, r.dtype) for r in results),
-        in_specs=specs,
-        out_specs=tuple(specs),
+        in_specs=[anywhere] * 4,
+        out_specs=(anywhere,) * 4,
+        scratch_shapes=[pltpu.VMEM(r.shape, r.dtype) for r in results] + [dma((4,)), dma((4,))],
         compiler_params=pltpu.CompilerParams(vmem_limit_bytes=60 * 1024 * 1024),
     )(*results)
     return (d_tokens, grad_gate[None], grad_up[None], grad_down[None])

time: 129 us -> 127 us (0.984)
  Pallas kernels: 128 us -> 126 us
    pallas_call x1, Pallas kernels: 4.04 us -> 2.69 us  [dense_shards(): pl.pallas_call(copy_kernel, out_shape=tuple((jax.ShapeDtypeStruct(r.shape...]
where the time goes in v6:
time: 127 us
  Pallas kernels  126 us (99%)
    pallas_call x1, Pallas kernels, dense_shards(): pl.pallas_call(fused_kernel, out_shape=(jax.ShapeDtypeStruct((tok_count,...  124 us
    pallas_call x1, Pallas kernels, dense_shards(): pl.pallas_call(copy_kernel, out_shape=tuple((jax.ShapeDtypeStruct(r.shape...  2.69 us

profile of v6, /device:TPU:25, one launch (start us, length us, event | category | flops | bytes accessed | tf_op | source)
XLA Modules:
  0.0 126.9 jit_solution(10200163302715535209)
XLA Ops:
  0.6 123.6 %shard_map.102 = (bf16[128,1024]{1,0:T(8,128)(2,1)}, bf16[1024,384]{1,0:T(8,128)(2,1)}, bf16[1024,384]{1,0:T(8,128)(2,1)}, bf16[384,1024]{1,0:T(8,128)(2,1)}) custom-call(bf16[128,1024]{1,0:T(8,128)(2,1)} %tok.1, bf16[128,1024]{1,0:T(8,128)(2,1)} %cot.1, s32[8,128]{1,0:T(8,128)} %bitcast.14, f32[8,128]{1,0:T(8,128)} %bitcast.15, bf16[1024,384]{1,0:T(8,128)(2,1)} %bitcast.8, ...), custom_call_target="tpu_custom_call" | custom-call | flops 12884901888 | bytes 8388608 | tf_op jit(solution)/shard_map/pallas_call | solution.py:476
  124.3 2.7 %shard_map.103 = (bf16[128,1024]{1,0:T(8,128)(2,1)}, bf16[1024,384]{1,0:T(8,128)(2,1)}, bf16[1024,384]{1,0:T(8,128)(2,1)}, bf16[384,1024]{1,0:T(8,128)(2,1)}) custom-call(bf16[128,1024]{1,0:T(8,128)(2,1)} %get-tuple-element.12.refs_0_, bf16[1024,384]{1,0:T(8,128)(2,1)} %get-tuple-element.13.refs_1_, bf16[1024,384]{1,0:T(8,128)(2,1)} %get-tuple-element.14.refs_2_, ...), custom_call_target="tpu_custom_call" | custom-call | tf_op jit(solution)/shard_map/pallas_call | solution.py:528

commit v7 on v6

--- a/solution.py
+++ b/solution.py
@@ -519,7 +519,7 @@
             dma((4, 3)), dma((4, 3)),
         ],
         compiler_params=pltpu.CompilerParams(
-            collective_id=0, has_side_effects=True, vmem_limit_bytes=60 * 1024 * 1024
+            collective_id=0, has_side_effects=True, vmem_limit_bytes=48 * 1024 * 1024
         ),
         cost_estimate=pl.CostEstimate(
             flops=16 * rows * 2 * feats * width, bytes_accessed=8 * 1024 * 1024, transcendentals=rows * width
@@ -531,7 +531,7 @@
         in_specs=[anywhere] * 4,
         out_specs=(anywhere,) * 4,
         scratch_shapes=[pltpu.VMEM(r.shape, r.dtype) for r in results] + [dma((4,)), dma((4,))],
-        compiler_params=pltpu.CompilerParams(vmem_limit_bytes=60 * 1024 * 1024),
+        compiler_params=pltpu.CompilerParams(vmem_limit_bytes=8 * 1024 * 1024),
     )(*results)
     return (d_tokens, grad_gate[None], grad_up[None], grad_down[None])
 

time: 127 us -> 130 us (1.024)
  local copies, waits for them, and re-layouts: 0 us -> 5.98 us
  Pallas kernels: 126 us -> 123 us
    unnamed x0 -> x14, local copies, waits for them, and re-layouts: none -> 5.98 us
    pallas_call x1, Pallas kernels: 124 us -> 121 us  [dense_shards(): pl.pallas_call(fused_kernel, out_shape=(jax.ShapeDtypeStruct((tok_count,...]
where the time goes in v7:
time: 130 us
  Pallas kernels  123 us (95%)
  local copies, waits for them, and re-layouts  5.98 us (5%)
    pallas_call x1, Pallas kernels, dense_shards(): pl.pallas_call(fused_kernel, out_shape=(jax.ShapeDtypeStruct((tok_count,...  121 us
    unnamed x14, local copies, waits for them, and re-layouts  5.98 us

profile of v7, /device:TPU:25, one launch (start us, length us, event | category | flops | bytes accessed | tf_op | source)
XLA Modules:
  0.0 129.8 jit_solution(578900222991572421)
XLA Ops:
  0.6 0.0 copy-start.6
  0.6 0.0 copy-start.5
  0.7 0.7 copy-done.6
  1.3 0.0 copy-done.5
  1.3 0.0 copy-start
  1.3 1.1 copy-done
  2.5 0.0 copy-start.1
  2.5 1.1 copy-done.1
  3.6 0.0 copy-start.2
  3.6 1.1 copy-done.2
  4.7 0.0 copy-start.3
  4.7 0.9 copy-done.3
  5.7 0.0 copy-start.4
  5.7 0.9 copy-done.4
  6.6 121.4 %shard_map.102 = (bf16[128,1024]{1,0:T(8,128)(2,1)S(1)}, bf16[1024,384]{1,0:T(8,128)(2,1)S(1)}, bf16[1024,384]{1,0:T(8,128)(2,1)S(1)}, bf16[384,1024]{1,0:T(8,128)(2,1)S(1)}) custom-call(bf16[128,1024]{1,0:T(8,128)(2,1)S(1)} %copy-done.3, bf16[128,1024]{1,0:T(8,128)(2,1)S(1)} %copy-done.4, s32[8,128]{1,0:T(8,128)S(1)} %bitcast.11, f32[8,128]{1,0:T(8,128)S(1)} %bitcast.12, ...), custom_call_target="tpu_custom_call" | custom-call | flops 12884901888 | bytes 8388608 | tf_op jit(solution)/shard_map/pallas_call | solution.py:476
  128.0 1.7 %shard_map.103 = (bf16[128,1024]{1,0:T(8,128)(2,1)}, bf16[1024,384]{1,0:T(8,128)(2,1)}, bf16[1024,384]{1,0:T(8,128)(2,1)}, bf16[384,1024]{1,0:T(8,128)(2,1)}) custom-call(bf16[128,1024]{1,0:T(8,128)(2,1)S(1)} %get-tuple-element.12.refs_0_, bf16[1024,384]{1,0:T(8,128)(2,1)S(1)} %get-tuple-element.13.refs_1_, bf16[1024,384]{1,0:T(8,128)(2,1)S(1)} %get-tuple-element.14.refs_2_, ...), custom_call_target="tpu_custom_call" | custom-call | tf_op jit(solution)/shard_map/pallas_call | solution.py:528
Async XLA Ops:
  0.6 0.7 copy-start.6
  0.6 0.7 copy-start.5
  1.3 1.1 copy-start
  2.5 1.1 copy-start.1
  3.6 1.1 copy-start.2
  4.7 0.9 copy-start.3
  5.7 0.9 copy-start.4
